TPU v7x, 32 devices: a whole 2x2x4 slice. The times are simulated.
32 devices in a mesh: pulse: 8 (over y, x, core), range: 4 (over z).
Axes of the slice: x: 2, y: 2, z: 4, core: 2. Of those that a mesh axis runs over, the one named last changes fastest.
Arguments:
- raw_echoes: bfloat16 [512, 4096], P(('pulse', 'range')), may hold values from -6 to 6
- range_taps: bfloat16 [2048, 2], replicated, may hold values from -0.09375 to 0.09375
- mig_offset: int32 [2048], replicated, may hold values from -56 to 56
- interp_band: int32 [2048], replicated, may hold values from 0 to 15
- interp_table: bfloat16 [16, 8], replicated, may hold values from -2 to 2
- azimuth_taps: bfloat16 [1024, 2], replicated, may hold values from -0.125 to 0.125
- geo_list: int32 [32, 8, 4], P(('pulse', 'range')), may hold values from 0 to 255, as said below
- geo_frac: float32 [32, 8, 4], P(('pulse', 'range')), may hold values from 0.1 to 1
Outputs:
- focused: bfloat16 [512, 4096], P(None, ('pulse', 'range'))
- geo_tiles: float32 [256, 1024], P(('pulse', 'range'))
Inputs may be any that keep to these rules, and one draw needn't show every extreme that they name: `geo_list`: each entry names a map tile of the patch's own range strip or of one of the two strips beside it; tile t belongs to strip t // 8.
All inputs are finite; a program needn't handle non-finite values.
Results may differ from a plain program's by a relative error of at most 0.005.
The roundings to bfloat16 on the way count: a program that leaves them out, or rounds other values in their place, can miss the bound.
Values may be sent and summed in bfloat16 or wider, within the bound.
A program may use at most 128 MiB of HBM per device.

v0:
```python
import jax
import jax.numpy as jnp
from jax import lax
from jax.sharding import PartitionSpec as P

MAXOFF = 56
LOOKS = 4


def with_halo(shard, sides, width):
    for axis, dim in sides:
        size, length = (lax.axis_size(axis), shard.shape[dim])
        up = [(i, (i + 1) % size) for i in range(size - 1)]
        down = [(j, i) for i, j in up]
        last = lax.slice_in_dim(shard, length - width, length, axis=dim)
        first = lax.slice_in_dim(shard, 0, width, axis=dim)
        before = lax.ppermute(last, axis, up)
        after = lax.ppermute(first, axis, down)
        shard = jnp.concatenate([before, shard, after], axis=dim)
    return shard


def passed_along(shard, axis, by):
    length = lax.axis_size(axis)
    pairs = [(i, i + by) for i in range(length) if 0 <= i + by < length]
    return lax.ppermute(shard, axis, pairs)


def toeplitz_block(vector, size):
    flipped = jnp.concatenate([vector[::-1], jnp.zeros((1,), vector.dtype)])
    tiled = jnp.tile(flipped, size)[: size * (2 * size - 1)].reshape(size, 2 * size - 1)
    return tiled[:, size - 1 : 2 * size - 1]


def range_matrices(range_taps, dtype):
    block = range_taps.shape[0] // 8
    taps = range_taps.astype(jnp.float32)
    padded = jnp.concatenate(
        [jnp.zeros((block - 1, 2), jnp.float32), taps, jnp.zeros((block, 2), jnp.float32)], 0
    )
    matrices = []
    for offset in range(9):
        window = padded[offset * block : offset * block + 2 * block - 1]
        real_part = toeplitz_block(window[:, 0], block)
        imag_part = toeplitz_block(window[:, 1], block)
        upper = jnp.stack([real_part, imag_part], -1)
        lower = jnp.stack([-imag_part, real_part], -1)
        matrices.append(jnp.stack([upper, lower], 1).reshape(2 * block, 2 * block).astype(dtype))
    return matrices


def azimuth_matrices(azimuth_taps, dtype):
    block = azimuth_taps.shape[0] // 4
    taps = azimuth_taps.astype(jnp.float32)
    padded = jnp.concatenate(
        [jnp.zeros((block - 1, 2), jnp.float32), taps, jnp.zeros((block, 2), jnp.float32)], 0
    )
    matrices = []
    for offset in range(5):
        window = padded[offset * block : offset * block + 2 * block - 1]
        joined = jnp.concatenate(
            [toeplitz_block(window[:, 0], block), toeplitz_block(window[:, 1], block)], 1
        )
        matrices.append(joined.astype(dtype))
    return matrices


def filter_lines(lines, matrices):
    breadth = matrices[0].shape[0]
    line_count = lines.shape[0]
    block_count = lines.shape[1] // breadth
    blocks = lines.reshape(line_count, block_count, breadth)
    padded = jnp.concatenate(
        [blocks, jnp.zeros((line_count, len(matrices) - 1, breadth), lines.dtype)], 1
    )
    summed = jnp.zeros((line_count * block_count, breadth), jnp.float32)
    for offset, matrix in enumerate(matrices):
        segment = padded[:, offset : offset + block_count].reshape(
            line_count * block_count, breadth
        )
        summed = summed + jnp.dot(segment, matrix, preferred_element_type=jnp.float32)
    return summed.reshape(line_count, block_count * breadth)


def compress(columns, matrices):
    block = matrices[0].shape[0]
    length = columns.shape[0]
    breadth = columns.shape[1]
    block_count = length // block
    blocks = columns.reshape(block_count, block, breadth)
    padded = jnp.concatenate(
        [blocks, jnp.zeros((len(matrices) - 1, block, breadth), columns.dtype)], 0
    )
    summed = jnp.zeros((block_count, 2 * block, breadth), jnp.float32)
    for offset, matrix in enumerate(matrices):
        summed = summed + jnp.einsum(
            "bmr,mn->bnr",
            padded[offset : offset + block_count],
            matrix,
            preferred_element_type=jnp.float32,
        )
    direct = summed[:, :block].reshape(block_count, block, breadth // 2, 2)
    crossed = summed[:, block:].reshape(block_count, block, breadth // 2, 2)
    real_part = direct[..., 0] - crossed[..., 1]
    imag_part = direct[..., 1] + crossed[..., 0]
    return jnp.stack([real_part, imag_part], -1).reshape(length, breadth)


def migrate_banded(windows, offsets, bands, table, lead):
    strip_count = windows.shape[1]
    breadth = windows.shape[2]
    bin_count = offsets.shape[0] // strip_count
    band_count = table.shape[0]
    tap_count = table.shape[1]
    selector = (bands[:, None] == jnp.arange(band_count, dtype=jnp.int32)[None, :]).astype(
        jnp.float32
    )
    kernels = jnp.dot(
        selector,
        table.astype(jnp.float32),
        precision=lax.Precision.HIGHEST,
        preferred_element_type=jnp.float32,
    )
    kernels = kernels.reshape(strip_count, bin_count, tap_count)
    column = jnp.arange(2 * bin_count, dtype=jnp.int32)
    parity = column % 2
    base = (
        jnp.arange(bin_count, dtype=jnp.int32)[None, :]
        + offsets.reshape(strip_count, bin_count)
        + (lead - tap_count // 2 + 1)
    )
    base_cols = jnp.repeat(base, 2, axis=1)
    window_pos = jnp.arange(breadth, dtype=jnp.int32)
    banded = jnp.zeros((strip_count, breadth, 2 * bin_count), jnp.float32)
    for tap_index in range(tap_count):
        source = (base_cols + tap_index) * 2 + parity[None, :]
        weights = jnp.repeat(kernels[:, :, tap_index], 2, axis=1)
        hit = window_pos[None, :, None] == source[:, None, :]
        banded = banded + jnp.where(hit, weights[:, None, :], 0.0)
    product = jnp.einsum(
        "psw,swc->psc", windows, banded.astype(jnp.bfloat16), preferred_element_type=jnp.float32
    )
    return product.reshape(windows.shape[0], strip_count * 2 * bin_count)


def body(
    raw_echoes, range_taps, mig_offset, interp_band, interp_table, azimuth_taps, geo_list, geo_frac
):
    strips = lax.axis_size("pulse") * lax.axis_size("range")
    strip_index = lax.axis_index(("pulse", "range"))
    pulse_rows = raw_echoes.shape[0]
    bins_here = raw_echoes.shape[1] // 2 // strips
    margin = MAXOFF + 4
    filtered = filter_lines(raw_echoes, range_matrices(range_taps, jnp.bfloat16)).astype(
        jnp.bfloat16
    )
    arranged = filtered.reshape(1, pulse_rows, strips, 2 * bins_here)
    turned = lax.all_to_all(arranged, ("pulse", "range"), split_axis=2, concat_axis=0, tiled=True)
    columns = turned.reshape(pulse_rows * strips, 2 * bins_here)
    widened = with_halo(columns, ((("pulse", "range"), 1),), 2 * margin)
    own_offsets = lax.dynamic_slice_in_dim(mig_offset, strip_index * bins_here, bins_here)
    own_bands = lax.dynamic_slice_in_dim(interp_band, strip_index * bins_here, bins_here)
    windows = widened.reshape(widened.shape[0], 1, widened.shape[1])
    migrated = migrate_banded(windows, own_offsets, own_bands, interp_table, margin).astype(
        jnp.bfloat16
    )
    focus = compress(migrated, azimuth_matrices(azimuth_taps, jnp.bfloat16))
    focused = focus.astype(jnp.bfloat16)
    power = focus.reshape(-1, LOOKS, bins_here, 2)
    looked = jnp.sum(power * power, axis=(1, 3)) / LOOKS
    patch_count = geo_list.shape[1]
    patches = looked.reshape(patch_count, -1)
    local_tiles = geo_list[0] - (strip_index - 1) * patch_count
    slots = jnp.arange(3 * patch_count, dtype=jnp.int32)
    spread = jnp.sum(
        jnp.where(local_tiles[None, :, :] == slots[:, None, None], geo_frac[0][None, :, :], 0.0),
        axis=2,
    )
    partial_value = jnp.dot(
        spread, patches, precision=lax.Precision.HIGHEST, preferred_element_type=jnp.float32
    )
    lower_part = partial_value[:patch_count]
    own_part = partial_value[patch_count : 2 * patch_count]
    upper_part = partial_value[2 * patch_count :]
    from_above = passed_along(lower_part.astype(jnp.bfloat16), ("pulse", "range"), -1).astype(
        lower_part.dtype
    )
    from_below = passed_along(upper_part, ("pulse", "range"), 1)
    return (focused, own_part + from_above + from_below)


def solution(mesh):
    placed = (
        P(("pulse", "range"), None),
        P(),
        P(),
        P(),
        P(),
        P(),
        P(("pulse", "range"), None, None),
        P(("pulse", "range"), None, None),
    )
    return jax.shard_map(
        body,
        mesh=mesh,
        in_specs=placed,
        out_specs=(P(None, ("pulse", "range")), P(("pulse", "range"), None)),
        check_vma=False,
    )
```

profile of v0, /device:TPU:1, one launch (start us, length us, event | category | flops | bytes accessed | tf_op | source)
XLA Modules:
  0.0 736.8 jit_solution(7529790359511026885)
XLA Ops:
  0.6 1.6 fusion.130
  3.5 0.7 convert_element_type.140
  8.1 0.8 fusion.32
  10.0 0.8 fusion.33
  10.8 0.8 fusion.42
  12.2 0.8 fusion.34
  14.1 0.8 fusion.35
  15.6 0.8 fusion.36
  16.3 0.8 fusion.45
  17.7 0.4 reshape.732
  18.4 23.2 %copy.120 = bf16[256,2,256,2]{3,2,1,0:T(8,128)(2,1)} copy(bf16[256,2,256,2]{2,0,3,1:T(8,128)(2,1)S(1)} %pad_maximum_fusion.1) | data formatting | bytes 1048576 | tf_op jit(solution)/shard_map/stack | solution.py:48
  41.6 49.6 %convert_element_type.142 = bf16[512,512]{1,0:T(8,128)(2,1)} reshape(bf16[256,2,256,2]{3,2,1,0:T(8,128)(2,1)} %copy.120) | data formatting | bytes 1048576 | tf_op jit(solution)/shard_map/convert_element_type | solution.py:48
  91.4 0.7 pad_slice_fusion.15
  92.2 0.7 pad_maximum_fusion.37
  93.0 0.4 reshape.728
  93.7 23.1 %copy.119 = bf16[256,2,256,2]{3,2,1,0:T(8,128)(2,1)} copy(bf16[256,2,256,2]{2,0,3,1:T(8,128)(2,1)S(1)} %pad_maximum_fusion) | data formatting | bytes 1048576 | tf_op jit(solution)/shard_map/stack | solution.py:48
  116.7 48.9 %convert_element_type.141 = bf16[512,512]{1,0:T(8,128)(2,1)S(1)} reshape(bf16[256,2,256,2]{3,2,1,0:T(8,128)(2,1)} %copy.119) | data formatting | bytes 1048576 | tf_op jit(solution)/shard_map/convert_element_type | solution.py:48
  165.7 0.7 reshape_reshape.4
  166.6 0.4 reshape.735
  167.3 23.1 %copy.122 = bf16[256,2,256,2]{3,2,1,0:T(8,128)(2,1)} copy(bf16[256,2,256,2]{2,0,3,1:T(8,128)(2,1)S(1)} %pad_maximum_fusion.2) | data formatting | bytes 1048576 | tf_op jit(solution)/shard_map/stack | solution.py:48
  190.3 48.9 %convert_element_type.143 = bf16[512,512]{1,0:T(8,128)(2,1)S(1)} reshape(bf16[256,2,256,2]{3,2,1,0:T(8,128)(2,1)} %copy.122) | data formatting | bytes 1048576 | tf_op jit(solution)/shard_map/convert_element_type | solution.py:48
  239.8 0.4 reshape.738
  240.5 23.1 %copy.124 = bf16[256,2,256,2]{3,2,1,0:T(8,128)(2,1)} copy(bf16[256,2,256,2]{2,0,3,1:T(8,128)(2,1)S(1)} %pad_maximum_fusion.3) | data formatting | bytes 1048576 | tf_op jit(solution)/shard_map/stack | solution.py:48
  263.5 48.9 %convert_element_type.144 = bf16[512,512]{1,0:T(8,128)(2,1)S(1)} reshape(bf16[256,2,256,2]{3,2,1,0:T(8,128)(2,1)} %copy.124) | data formatting | bytes 1048576 | tf_op jit(solution)/shard_map/convert_element_type | solution.py:48
  312.6 0.4 reshape.741
  313.3 23.1 %copy.126 = bf16[256,2,256,2]{3,2,1,0:T(8,128)(2,1)} copy(bf16[256,2,256,2]{2,0,3,1:T(8,128)(2,1)S(1)} %pad_maximum_fusion.4) | data formatting | bytes 1048576 | tf_op jit(solution)/shard_map/stack | solution.py:48
  336.4 49.1 %convert_element_type.145 = bf16[512,512]{1,0:T(8,128)(2,1)S(1)} reshape(bf16[256,2,256,2]{3,2,1,0:T(8,128)(2,1)} %copy.126) | data formatting | bytes 1048576 | tf_op jit(solution)/shard_map/convert_element_type | solution.py:48
  386.1 0.4 reshape.744
  386.6 1.0 maximum_bitcast_fusion.10
  387.7 23.1 %copy.128 = bf16[256,2,256,2]{3,2,1,0:T(8,128)(2,1)} copy(bf16[256,2,256,2]{2,0,3,1:T(8,128)(2,1)S(1)} %pad_maximum_fusion.5) | data formatting | bytes 1048576 | tf_op jit(solution)/shard_map/stack | solution.py:48
  410.8 49.6 %convert_element_type.146 = bf16[512,512]{1,0:T(8,128)(2,1)} reshape(bf16[256,2,256,2]{3,2,1,0:T(8,128)(2,1)} %copy.128) | data formatting | bytes 1048576 | tf_op jit(solution)/shard_map/convert_element_type | solution.py:48
  460.5 0.4 reshape.747
  461.0 0.9 maximum_bitcast_fusion.12
  462.1 23.1 %copy.130 = bf16[256,2,256,2]{3,2,1,0:T(8,128)(2,1)} copy(bf16[256,2,256,2]{2,0,3,1:T(8,128)(2,1)S(1)} %pad_maximum_fusion.6) | data formatting | bytes 1048576 | tf_op jit(solution)/shard_map/stack | solution.py:48
  485.1 49.6 %convert_element_type.147 = bf16[512,512]{1,0:T(8,128)(2,1)} reshape(bf16[256,2,256,2]{3,2,1,0:T(8,128)(2,1)} %copy.130) | data formatting | bytes 1048576 | tf_op jit(solution)/shard_map/convert_element_type | solution.py:48
  535.3 0.4 reshape.750
  536.0 23.1 %copy.132 = bf16[256,2,256,2]{3,2,1,0:T(8,128)(2,1)} copy(bf16[256,2,256,2]{2,0,3,1:T(8,128)(2,1)S(1)} %pad_maximum_fusion.7) | data formatting | bytes 1048576 | tf_op jit(solution)/shard_map/stack | solution.py:48
  559.0 49.6 %convert_element_type.148 = bf16[512,512]{1,0:T(8,128)(2,1)} reshape(bf16[256,2,256,2]{3,2,1,0:T(8,128)(2,1)} %copy.132) | data formatting | bytes 1048576 | tf_op jit(solution)/shard_map/convert_element_type | solution.py:48
  608.7 0.4 reshape.753
  609.5 23.1 %copy.134 = bf16[256,2,256,2]{3,2,1,0:T(8,128)(2,1)} copy(bf16[256,2,256,2]{2,0,3,1:T(8,128)(2,1)S(1)} %pad_maximum_fusion.8) | data formatting | bytes 1048576 | tf_op jit(solution)/shard_map/stack | solution.py:48
  632.6 49.3 %convert_element_type.149 = bf16[512,512]{1,0:T(8,128)(2,1)S(1)} reshape(bf16[256,2,256,2]{3,2,1,0:T(8,128)(2,1)} %copy.134) | data formatting | bytes 1048576 | tf_op jit(solution)/shard_map/convert_element_type | solution.py:48
  683.7 1.4 convolution_add_fusion.3
  685.1 1.4 convolution_add_fusion.2
  686.5 1.4 convolution_add_fusion.1
  688.4 0.7 copy.137
  689.1 7.1 all-to-all-start
  696.4 0.8 add_multiply_fusion.7
  698.9 0.8 dynamic_slice.7
  701.6 0.4 reshape.760
  702.8 0.4 reshape.761
  705.9 0.4 reshape.757
  706.6 0.4 reshape.756
  708.0 0.4 reshape.725
  709.3 0.4 reshape.759
  710.7 0.4 reshape.763
  711.6 3.3 collective-permute-start
  714.9 4.2 collective-permute-start.1
  719.4 1.1 collective-permute-done
  720.4 3.6 collective-permute-done.1
  724.1 0.5 fusion.1
  727.6 2.2 collective-permute-start.3
  729.8 5.2 collective-permute-start.2
  735.3 0.8 copy.145
  736.0 0.6 fusion.88
  (305 shorter events, 29.5 us)
Async XLA Ops:
  0.6 699.0 %copy-start = (bf16[16,8]{0,1:T(8,128)(2,1)S(1)}, bf16[16,8]{0,1:T(8,128)(2,1)}, u32[]{:S(2)}) copy-start(bf16[16,8]{0,1:T(8,128)(2,1)} %param.12) | copy-start | bytes 772
  18.4 73.0 %copy-start.8 = (bf16[1024,2]{0,1:T(2,128)(2,1)S(1)}, bf16[1024,2]{0,1:T(2,128)(2,1)}, u32[]{:S(2)}) copy-start(bf16[1024,2]{0,1:T(2,128)(2,1)} %param.13) | copy-start | bytes 12292
  93.7 72.0 %copy-start.7 = (bf16[16,4096]{1,0:T(8,128)(2,1)S(1)}, bf16[16,4096]{1,0:T(8,128)(2,1)}, u32[]{:S(2)}) copy-start(bf16[16,4096]{1,0:T(8,128)(2,1)} %param.8) | copy-start | bytes 393220
  240.5 72.7 %copy-start.5 = (bf16[256,256,1]{1,0,2:T(8,128)(2,1)S(1)}, bf16[256,256,1]{1,0,2:T(8,128)(2,1)}, u32[]{:S(2)}) copy-start(bf16[256,256,1]{1,0,2:T(8,128)(2,1)} %fusion.32) | copy-start | bytes 393220
  313.3 72.2 %copy-start.10 = (f32[511,1]{0,1:T(1,128)S(1)}, f32[511,1]{0,1:T(1,128)}, u32[]{:S(2)}) copy-start(f32[511,1]{0,1:T(1,128)} %get-tuple-element.55) | copy-start | bytes 6136
  462.1 73.8 %copy-start.4 = (bf16[256,256,1]{1,0,2:T(8,128)(2,1)S(1)}, bf16[256,256,1]{1,0,2:T(8,128)(2,1)}, u32[]{:S(2)}) copy-start(bf16[256,256,1]{1,0,2:T(8,128)(2,1)} %fusion.35) | copy-start | bytes 393220
  535.9 73.4 %copy-start.2 = (bf16[256,256,1]{1,0,2:T(8,128)(2,1)S(1)}, bf16[256,256,1]{1,0,2:T(8,128)(2,1)}, u32[]{:S(2)}) copy-start(bf16[256,256,1]{1,0,2:T(8,128)(2,1)} %fusion.45) | copy-start | bytes 393220
  536.0 73.4 %copy-start.3 = (bf16[256,256,1]{1,0,2:T(8,128)(2,1)S(1)}, bf16[256,256,1]{1,0,2:T(8,128)(2,1)}, u32[]{:S(2)}) copy-start(bf16[256,256,1]{1,0,2:T(8,128)(2,1)} %fusion.36) | copy-start | bytes 393220
  609.4 72.5 %copy-start.6 = (bf16[128,512]{1,0:T(8,128)(2,1)S(1)}, bf16[128,512]{1,0:T(8,128)(2,1)}, u32[]{:S(2)}) copy-start(bf16[128,512]{1,0:T(8,128)(2,1)} %reshape_reshape.4) | copy-start | bytes 393220
  609.4 72.8 %copy-start.1 = (bf16[512,512]{1,0:T(8,128)(2,1)S(1)}, bf16[512,512]{1,0:T(8,128)(2,1)}, u32[]{:S(2)}) copy-start(bf16[512,512]{1,0:T(8,128)(2,1)} %convert_element_type.142) | copy-start | bytes 1572868
  609.5 86.8 %copy-start.9 = (bf16[1024,2]{0,1:T(2,128)(2,1)S(1)}, bf16[1024,2]{0,1:T(2,128)(2,1)}, u32[]{:S(2)}) copy-start(bf16[1024,2]{0,1:T(2,128)(2,1)} %param.13) | copy-start | bytes 12292
  609.5 91.1 %copy-start.13 = (f32[511,1]{0,1:T(1,128)S(1)}, f32[511,1]{0,1:T(1,128)}, u32[]{:S(2)}) copy-start(f32[511,1]{0,1:T(1,128)} %get-tuple-element.47) | copy-start | bytes 6136
  609.5 91.4 %copy-start.14 = (bf16[512]{0:T(512)(128)(2,1)S(1)}, bf16[512]{0:T(512)(128)(2,1)}, u32[]{:S(2)}) copy-start(bf16[512]{0:T(512)(128)(2,1)} %get-tuple-element.102) | copy-start | bytes 3076
  609.5 92.8 %copy-start.12 = (f32[511,1]{0,1:T(1,128)S(1)}, f32[511,1]{0,1:T(1,128)}, u32[]{:S(2)}) copy-start(f32[511,1]{0,1:T(1,128)} %get-tuple-element.49) | copy-start | bytes 6136
  632.6 70.8 %copy-start.11 = (f32[511,1]{0,1:T(1,128)S(1)}, f32[511,1]{0,1:T(1,128)}, u32[]{:S(2)}) copy-start(f32[511,1]{0,1:T(1,128)} %get-tuple-element.48) | copy-start | bytes 6136
  632.6 71.2 %copy-start.15 = (s32[1,8,4]{1,2,0:T(4,128)S(1)}, s32[1,8,4]{1,2,0:T(4,128)}, u32[]{:S(2)}) copy-start(s32[1,8,4]{1,2,0:T(4,128)} %param.14) | copy-start | bytes 388
  632.6 71.4 %copy-start.16 = (f32[1,8,4]{1,2,0:T(4,128)S(1)}, f32[1,8,4]{1,2,0:T(4,128)}, u32[]{:S(2)}) copy-start(f32[1,8,4]{1,2,0:T(4,128)} %param.15) | copy-start | bytes 388
  689.1 22.3 %all-to-all-start = ((bf16[1,16,32,128]{3,1,0,2:T(8,128)(2,1)}), bf16[1,16,32,128]{3,1,0,2:T(8,128)(2,1)S(1)}, u32[]{:S(2)}, u32[]{:S(2)}) async-start(bf16[1,16,32,128]{3,1,0,2:T(8,128)(2,1)} %copy.137), calls=%async_computation | async-start | bytes 262144 | tf_op jit(solution)/shard_map/all_to_all | solution.py:158
  711.6 8.8 %collective-permute-start = (bf16[512,120]{1,0:T(8,128)(2,1)S(1)}, bf16[512,120]{1,0:T(8,128)(2,1)S(1)}, u32[]{:S(2)}, u32[]{:S(2)}) collective-permute-start(bf16[512,120]{1,0:T(8,128)(2,1)S(1)} %get-tuple-element.22), channel_id=1, source_target_pairs={{0,1},{1,2},{2,3},{3,4},{4,5},{5,6},{6,7},{7,8},{8,9},{9,10},{10,1... | collective-permute-start | bytes 368648 | tf_op jit(solution)/shard_map/ppermute | solution.py:17
  714.9 9.2 %collective-permute-start.1 = (bf16[512,120]{1,0:T(8,128)(2,1)S(1)}, bf16[512,120]{1,0:T(8,128)(2,1)S(1)}, u32[]{:S(2)}, u32[]{:S(2)}) collective-permute-start(bf16[512,120]{1,0:T(8,128)(2,1)S(1)} %get-tuple-element.23), channel_id=1, source_target_pairs={{1,0},{2,1},{3,2},{4,3},{5,4},{6,5},{7,6},{8,7},{9,8},{10,9},{11,1... | collective-permute-start | bytes 368648 | tf_op jit(solution)/shard_map/ppermute | solution.py:18
  727.6 8.4 %collective-permute-start.3 = (f32[8,1024]{1,0:T(8,128)S(1)}, f32[8,1024]{1,0:T(8,128)S(1)}, u32[]{:S(2)}, u32[]{:S(2)}) collective-permute-start(f32[8,1024]{1,0:T(8,128)S(1)} %slice.597), channel_id=1, source_target_pairs={{0,1},{1,2},{2,3},{3,4},{4,5},{5,6},{6,7},{7,8},{8,9},{9,10},{10,1... | collective-permute-start | bytes 98312 | tf_op jit(solution)/shard_map/ppermute | solution.py:26
  729.8 6.2 collective-permute-start.2
where the time goes:
time: 746 us; the launch traced here: 737 us
  local copies, waits for them, and re-layouts  689 us (92%)
  starting transfers between devices  22 us (3%)
  other arithmetic  9.91 us (1%)
  matrix products  8.34 us (1%)
    convert_element_type x9, local copies, waits for them, and re-layouts, range_matrices(): jnp.stack([upper, lower], 1).reshape(2 * block, 2 * block).astype(dtype)  443 us
    another operation x9, local copies, waits for them, and re-layouts, range_matrices(): jnp.stack([upper, lower], 1).reshape(2 * block, 2 * block).astype(dtype)  208 us
  transfers between devices with their start and end apart: 5, of which 2 were waited for; matrix products, arithmetic and copies ran while one was open for 2% of the time, Pallas kernels for 0%

commit v1 on v0

v1 whole, which is shorter than its diff:
```python
import functools

import jax
import jax.numpy as jnp
from jax import lax
from jax.experimental import pallas as pl
from jax.experimental.pallas import tpu as pltpu
from jax.sharding import PartitionSpec as P

LOOKS = 4
PROWS = 16
LANES = 128
GROUP = 16
MESH = pl.DeviceIdType.MESH


def iota(shape, dim):
    return lax.broadcasted_iota(jnp.int32, shape, dim)


def shifted_rows(taps, width):
    have = min(width, taps.shape[1])
    line = taps[:, :have].astype(jnp.float32)
    if have < width:
        line = jnp.concatenate([line, jnp.zeros((1, width - have), jnp.float32)], 1)
    eight = jnp.broadcast_to(line, (8, width))
    row = iota((8, width), 0)
    for bit in (1, 2, 4):
        eight = jnp.where((row & bit) != 0, pltpu.roll(eight, bit, 1), eight)
    for step in range(LANES // 16):
        halves = []
        for start in (16 * step, 16 * step + 8):
            moved = eight if start == 0 else pltpu.roll(eight, start, 1)
            keep = iota((8, LANES), 1) >= iota((8, LANES), 0) + start
            first = jnp.where(keep, moved[:, :LANES], 0.0)
            halves.append(jnp.concatenate([first, moved[:, LANES:]], 1))
        yield step, jnp.concatenate(halves, 0)


def kernel(
    devices,
    across,
    raw_ref,
    rtaps_ref,
    offset_ref,
    band_ref,
    table_ref,
    ataps_ref,
    list_ref,
    frac_ref,
    focused_ref,
    tiles_ref,
    zr_ref,
    zi_ref,
    zn_ref,
    za_ref,
    x_ref,
    sum_ref,
    f_ref,
    b_ref,
    send_ref,
    recv_ref,
    power_ref,
    low_ref,
    high_ref,
    from_next_ref,
    from_prev_ref,
    send_sem,
    recv_sem,
    low_send_sem,
    high_send_sem,
    low_recv_sem,
    high_recv_sem,
):
    pulse_at, range_at = lax.axis_index("pulse"), lax.axis_index("range")
    me = pulse_at * across + range_at
    rows, breadth = raw_ref.shape
    chunks = breadth // (2 * LANES)
    groups = chunks // GROUP
    pulses = devices * rows
    patches = list_ref.shape[1]
    rwidth = zr_ref.shape[1]
    awidth = za_ref.shape[1]

    def place(index):
        return (lax.div(index, across), lax.rem(index, across))

    barrier = pltpu.get_barrier_semaphore()

    def greet(distance, carry):
        other = lax.rem(me + distance, devices)
        pl.semaphore_signal(barrier, inc=1, device_id=place(other), device_id_type=MESH)
        return carry

    lax.fori_loop(1, devices, greet, 0)

    def each_group(body):
        if groups == 1:
            body(0)
        else:
            lax.fori_loop(0, groups, lambda g, c: (body(g * GROUP), c)[1], 0)

    side = (2 * LANES, 2 * LANES)
    column = iota(side, 1)
    source = 2 * (LANES - 1 - (column % LANES)) + column // LANES
    parts_apart = (iota(side, 0) == source).astype(jnp.float32).astype(jnp.bfloat16)
    lines = jnp.concatenate(
        [raw_ref[:, 2 * LANES * j : 2 * LANES * (j + 1)] for j in range(chunks)], 0
    )
    x_ref[0 : chunks * rows, :] = jnp.dot(
        lines, parts_apart, preferred_element_type=jnp.float32
    ).astype(jnp.bfloat16)
    spare = x_ref.shape[0] - chunks * rows
    if spare:
        x_ref[chunks * rows :, :] = jnp.zeros((spare, 2 * LANES), jnp.bfloat16)

    for step, real_rows in shifted_rows(rtaps_ref[0:1, :], rwidth):
        zr_ref[16 * step : 16 * step + 16, :] = real_rows.astype(jnp.bfloat16)
    for step, imag_rows in shifted_rows(rtaps_ref[1:2, :], rwidth):
        zi_ref[16 * step : 16 * step + 16, :] = imag_rows.astype(jnp.bfloat16)
        zn_ref[16 * step : 16 * step + 16, :] = (-imag_rows).astype(jnp.bfloat16)

    def range_group(first):
        for apart in range(rwidth // LANES):
            count = GROUP - apart if groups == 1 else GROUP
            if count <= 0:
                continue
            at = slice(LANES * apart, LANES * (apart + 1))
            zr, zi, zn = zr_ref[:, at], zi_ref[:, at], zn_ref[:, at]
            weights = jnp.concatenate(
                [jnp.concatenate([zr, zi], 1), jnp.concatenate([zn, zr], 1)], 0
            )
            start = pl.multiple_of((first + apart) * rows, 16)
            product = jnp.dot(
                x_ref[pl.ds(start, count * rows), :],
                weights,
                preferred_element_type=jnp.float32,
            )
            if apart == 0:
                sum_ref[...] = product
            else:
                sum_ref[0 : count * rows, :] += product
        start = pl.multiple_of((first + 1) * rows, 16)
        f_ref[pl.ds(start, GROUP * rows), :] = sum_ref[...].astype(jnp.bfloat16)

    f_ref[0:rows, :] = jnp.zeros((rows, 2 * LANES), jnp.bfloat16)
    f_ref[(chunks + 1) * rows :, :] = jnp.zeros((rows, 2 * LANES), jnp.bfloat16)
    each_group(range_group)

    window = (2 * LANES, LANES)
    lane = iota(window, 0) % LANES
    shift = jnp.where(lane < LANES // 2, -LANES, LANES)
    bin_of = LANES - 1 - lane + jnp.where(iota(window, 0) < LANES, 0, shift)
    delta = bin_of - iota(window, 1) + 3
    taps = table_ref.shape[0]
    bands = table_ref.shape[1]
    table = table_ref[...]
    left = iota((rows, LANES), 1) < LANES // 2

    def migrate_group(first):
        for j in range(GROUP):
            at = pl.multiple_of((first + j) * LANES, LANES)
            offsets = offset_ref[:, pl.ds(at, LANES)]
            chosen = band_ref[:, pl.ds(at, LANES)]
            onehot = (iota((bands, LANES), 0) == chosen).astype(jnp.float32).astype(jnp.bfloat16)
            weights = jnp.dot(table, onehot, preferred_element_type=jnp.float32)
            banded = jnp.zeros(window, jnp.float32)
            for tap in range(taps):
                banded = jnp.where(delta == offsets + tap, weights[tap : tap + 1, :], banded)
            b_ref[j] = banded.astype(jnp.bfloat16)
        for j in range(GROUP):
            start = pl.multiple_of((first + j) * rows, 16)
            before = f_ref[pl.ds(start, rows), :]
            here = f_ref[pl.ds(pl.multiple_of(start + rows, 16), rows), :]
            after = f_ref[pl.ds(pl.multiple_of(start + 2 * rows, 16), rows), :]
            both = []
            for part in (slice(0, LANES), slice(LANES, 2 * LANES)):
                around = jnp.where(left, before[:, part], after[:, part])
                both.append(jnp.concatenate([here[:, part], around], 1))
            moved = jnp.dot(
                jnp.concatenate(both, 0), b_ref[j], preferred_element_type=jnp.float32
            )
            real_part, imag_part = moved[:rows], moved[rows:]
            even = jnp.where(left, real_part, pltpu.roll(imag_part, LANES // 2, 1))
            odd = jnp.where(left, pltpu.roll(real_part, LANES // 2, 1), imag_part)
            send_ref[2 * (first + j)] = even.astype(jnp.bfloat16)
            send_ref[2 * (first + j) + 1] = odd.astype(jnp.bfloat16)

    each_group(migrate_group)

    pl.semaphore_wait(barrier, devices - 1)

    def send(distance, carry):
        other = lax.rem(me + distance, devices)
        pltpu.make_async_remote_copy(
            src_ref=send_ref.at[other],
            dst_ref=recv_ref.at[me],
            send_sem=send_sem,
            recv_sem=recv_sem,
            device_id=place(other),
            device_id_type=MESH,
        ).start()
        return carry

    lax.fori_loop(1, devices, send, 0)
    recv_ref[me] = send_ref[me]

    for step, real_rows in shifted_rows(ataps_ref[0:1, :], awidth):
        za_ref[16 * step : 16 * step + 16, :] = real_rows.astype(jnp.bfloat16)
    for step, imag_rows in shifted_rows(ataps_ref[1:2, :], awidth):
        za_ref[LANES + 16 * step : LANES + 16 * step + 16, :] = imag_rows.astype(jnp.bfloat16)

    base = (me - 1) * patches
    slot = iota((3 * patches, patches), 0) + base
    spread = jnp.zeros((3 * patches, patches), jnp.float32)
    for over in range(list_ref.shape[0]):
        spread += jnp.where(
            list_ref[over : over + 1, :] == slot, frac_ref[over : over + 1, :], 0.0
        )

    square = (LANES, LANES)
    column = iota(square, 1)
    parts_beside = (iota(square, 0) == LANES // 2 * (column % 2) + column // 2)
    parts_beside = parts_beside.astype(jnp.float32).astype(jnp.bfloat16)
    sign = jnp.where(iota(square, 1) < LANES // 2, -1.0, 1.0)

    others = pl.ds(0, devices - 1)
    pltpu.make_async_copy(recv_ref.at[others], recv_ref.at[others], recv_sem).wait()

    for block in range(pulses // LANES):
        depth = min(awidth, pulses - LANES * block)
        first = LANES * block // rows
        columns = recv_ref[first : first + depth // rows].reshape(depth, LANES)
        product = jnp.dot(za_ref[:, :depth], columns, preferred_element_type=jnp.float32)
        focus = product[:LANES] + sign * pltpu.roll(product[LANES:], LANES // 2, 1)
        at = slice(LANES * block, LANES * (block + 1))
        focused_ref[at, :] = jnp.dot(
            focus.astype(jnp.bfloat16), parts_beside, preferred_element_type=jnp.float32
        ).astype(jnp.bfloat16)
        power_ref[at, :] = focus * focus

    stride = LOOKS * PROWS
    left_half = iota((patches, LANES), 1) < LANES // 2
    pieces = []
    for piece in range(stride // (2 * LOOKS)):
        summed = []
        for half in range(2):
            start = 2 * LOOKS * piece + LOOKS * half
            total = power_ref[pl.ds(start, patches, stride=stride), :]
            for look in range(1, LOOKS):
                total += power_ref[pl.ds(start + look, patches, stride=stride), :]
            summed.append(total + pltpu.roll(total, LANES // 2, 1))
        pieces.append(jnp.where(left_half, summed[0], summed[1]) * (1.0 / LOOKS))
    looked = jnp.concatenate(pieces, 1)
    partial = jnp.dot(
        spread, looked, precision=lax.Precision.HIGHEST, preferred_element_type=jnp.float32
    )
    low_ref[...] = partial[:patches]
    high_ref[...] = partial[2 * patches :]

    def low_copy():
        return pltpu.make_async_remote_copy(
            src_ref=low_ref,
            dst_ref=from_next_ref,
            send_sem=low_send_sem,
            recv_sem=low_recv_sem,
            device_id=place(jnp.maximum(me - 1, 0)),
            device_id_type=MESH,
        )

    def high_copy():
        return pltpu.make_async_remote_copy(
            src_ref=high_ref,
            dst_ref=from_prev_ref,
            send_sem=high_send_sem,
            recv_sem=high_recv_sem,
            device_id=place(jnp.minimum(me + 1, devices - 1)),
            device_id_type=MESH,
        )

    @pl.when(me > 0)
    def _():
        low_copy().start()

    @pl.when(me < devices - 1)
    def _():
        high_copy().start()

    tiles_ref[...] = partial[patches : 2 * patches]
    pltpu.make_async_copy(send_ref.at[others], send_ref.at[others], send_sem).wait()

    @pl.when(me < devices - 1)
    def _():
        low_copy().wait_recv()
        tiles_ref[...] += from_next_ref[...]

    @pl.when(me > 0)
    def _():
        high_copy().wait_recv()
        tiles_ref[...] += from_prev_ref[...]

    @pl.when(me > 0)
    def _():
        low_copy().wait_send()

    @pl.when(me < devices - 1)
    def _():
        high_copy().wait_send()


def body(
    raw_echoes, range_taps, mig_offset, interp_band, interp_table, azimuth_taps, geo_list, geo_frac
):
    across = lax.axis_size("range")
    devices = lax.axis_size("pulse") * across
    rows, breadth = raw_echoes.shape
    pulses = rows * devices
    bins = breadth // 2
    chunks = bins // LANES
    patches = geo_list.shape[1]
    tile = PROWS * (bins // devices)
    rwidth = min(bins, range_taps.shape[0] + LANES)
    awidth = min(pulses, azimuth_taps.shape[0] + LANES)
    spare = 0 if chunks == GROUP else rwidth // LANES
    whole = pl.BlockSpec(memory_space=pltpu.VMEM)
    scratch = [
        pltpu.VMEM((LANES, rwidth), jnp.bfloat16),
        pltpu.VMEM((LANES, rwidth), jnp.bfloat16),
        pltpu.VMEM((LANES, rwidth), jnp.bfloat16),
        pltpu.VMEM((2 * LANES, awidth), jnp.bfloat16),
        pltpu.VMEM(((chunks + spare) * rows, 2 * LANES), jnp.bfloat16),
        pltpu.VMEM((GROUP * rows, 2 * LANES), jnp.float32),
        pltpu.VMEM(((chunks + 2) * rows, 2 * LANES), jnp.bfloat16),
        pltpu.VMEM((GROUP, 2 * LANES, LANES), jnp.bfloat16),
        pltpu.VMEM((devices, rows, LANES), jnp.bfloat16),
        pltpu.VMEM((devices, rows, LANES), jnp.bfloat16),
        pltpu.VMEM((pulses, LANES), jnp.float32),
        pltpu.VMEM((patches, tile), jnp.float32),
        pltpu.VMEM((patches, tile), jnp.float32),
        pltpu.VMEM((patches, tile), jnp.float32),
        pltpu.VMEM((patches, tile), jnp.float32),
    ] + [pltpu.SemaphoreType.DMA] * 6
    return pl.pallas_call(
        functools.partial(kernel, devices, across),
        out_shape=(
            jax.ShapeDtypeStruct((pulses, breadth // devices), jnp.bfloat16),
            jax.ShapeDtypeStruct((patches, tile), jnp.float32),
        ),
        in_specs=[whole] * 8,
        out_specs=(whole, whole),
        scratch_shapes=scratch,
        compiler_params=pltpu.CompilerParams(
            collective_id=0, has_side_effects=True, vmem_limit_bytes=40 * 2**20
        ),
    )(
        raw_echoes,
        range_taps.T,
        mig_offset.reshape(1, bins),
        interp_band.reshape(1, bins),
        interp_table.T,
        azimuth_taps.T,
        geo_list[0].T,
        geo_frac[0].T,
    )


def solution(mesh):
    placed = (
        P(("pulse", "range"), None),
        P(),
        P(),
        P(),
        P(),
        P(),
        P(("pulse", "range"), None, None),
        P(("pulse", "range"), None, None),
    )
    return jax.shard_map(
        body,
        mesh=mesh,
        in_specs=placed,
        out_specs=(P(None, ("pulse", "range")), P(("pulse", "range"), None)),
        check_vma=False,
    )
```

time: 746 us -> 24.4 us (0.03); the launches traced: 737 us -> 24.1 us
  local copies, waits for them, and re-layouts: 689 us -> 6.3 us
  starting transfers between devices: 22 us -> 0 us
  Pallas kernels: 0 us -> 17.1 us
  other arithmetic: 9.91 us -> 0 us
  matrix products: 8.34 us -> 0 us
    convert_element_type x14 -> x0, local copies, waits for them, and re-layouts: 444 us -> none  [the longest x9 443 us: range_matrices(): jnp.stack([upper, lower], 1).reshape(2 * block, 2 * block).astype(dtype)]
    another operation x29 -> x0, local copies, waits for them, and re-layouts: 214 us -> none  [the longest x9 208 us: range_matrices(): jnp.stack([upper, lower], 1).reshape(2 * block, 2 * block).astype(dtype)]
    pallas_call x0 -> x1, Pallas kernels: none -> 17.1 us  [body(): pl.pallas_call(functools.partial(kernel, devices, across), out_shape=(jax...]
    ppermute x4 -> x0, starting transfers between devices: 14.9 us -> none  [the longest x2 7.36 us: passed_along(): return lax.ppermute(shard, axis, pairs)]
    reshape x30 -> x0, local copies, waits for them, and re-layouts: 12.3 us -> none  [the longest x28 12 us: toeplitz_block(): jnp.tile(flipped, size)[:size * (2 * size - 1)].reshape(size, 2 * size - 1)]
  transfers between devices with their start and end apart: 5 -> 0, of which waited for: 2 -> 0; matrix products, arithmetic and copies ran while one was open for 2% -> 0% of each run, Pallas kernels for 0% -> 0%
where the time goes in v1:
time: 24.4 us; the launch traced here: 24.1 us
  Pallas kernels  17.1 us (70%)
  local copies, waits for them, and re-layouts  6.3 us (26%)
  between operations  0.66 us (3%)
    pallas_call x1, Pallas kernels, body(): pl.pallas_call(functools.partial(kernel, devices, across), out_shape=(jax...  17.1 us
    unnamed x18, local copies, waits for them, and re-layouts  6.3 us

profile of v1, /device:TPU:1, one launch (start us, length us, event | category | flops | bytes accessed | tf_op | source)
XLA Modules:
  0.0 24.1 jit_solution(8959999148445749696)
XLA Ops:
  0.6 0.0 copy-start.1
  0.6 0.0 copy-start.4
  0.7 0.7 %copy-done.1 = bf16[2048,2]{0,1:T(2,128)(2,1)S(1)} copy-done((bf16[2048,2]{0,1:T(2,128)(2,1)S(1)}, bf16[2048,2]{0,1:T(2,128)(2,1)}, u32[]{:S(2)}) %copy-start.1) | copy-done | bytes 8216
  1.3 0.0 copy-done.4
  1.3 0.0 copy-start
  1.3 0.9 %copy-done = bf16[16,4096]{1,0:T(8,128)(2,1)S(1)} copy-done((bf16[16,4096]{1,0:T(8,128)(2,1)S(1)}, bf16[16,4096]{1,0:T(8,128)(2,1)}, u32[]{:S(2)}) %copy-start) | copy-done | bytes 131096
  2.2 0.0 copy-start.2
  2.2 0.7 %copy-done.2 = s32[2048]{0:T(1024)S(1)} copy-done((s32[2048]{0:T(1024)S(1)}, s32[2048]{0:T(1024)}, u32[]{:S(2)}) %copy-start.2) | copy-done | bytes 8216
  2.9 0.0 copy-start.3
  2.9 0.7 %copy-done.3 = s32[2048]{0:T(1024)S(1)} copy-done((s32[2048]{0:T(1024)S(1)}, s32[2048]{0:T(1024)}, u32[]{:S(2)}) %copy-start.3) | copy-done | bytes 8216
  3.6 0.0 copy-start.5
  3.6 0.7 %copy-done.5 = bf16[16,8]{0,1:T(8,128)(2,1)S(1)} copy-done((bf16[16,8]{0,1:T(8,128)(2,1)S(1)}, bf16[16,8]{0,1:T(8,128)(2,1)}, u32[]{:S(2)}) %copy-start.5) | copy-done | bytes 280
  4.3 0.0 copy-start.6
  4.3 0.7 %copy-done.6 = s32[1,8,4]{1,2,0:T(4,128)S(1)} copy-done((s32[1,8,4]{1,2,0:T(4,128)S(1)}, s32[1,8,4]{1,2,0:T(4,128)}, u32[]{:S(2)}) %copy-start.6) | copy-done | bytes 152
  5.0 0.0 copy-start.7
  5.0 0.7 %copy-done.7 = f32[1,8,4]{1,2,0:T(4,128)S(1)} copy-done((f32[1,8,4]{1,2,0:T(4,128)S(1)}, f32[1,8,4]{1,2,0:T(4,128)}, u32[]{:S(2)}) %copy-start.7) | copy-done | bytes 152
  5.7 17.1 %shard_map.95 = (bf16[512,128]{1,0:T(8,128)(2,1)S(1)}, f32[8,1024]{1,0:T(8,128)S(1)}) custom-call(bf16[16,4096]{1,0:T(8,128)(2,1)S(1)} %copy-done, bf16[2,2048]{1,0:T(2,128)(2,1)S(1)} %bitcast.11, s32[1,2048]{1,0:T(1,128)S(1)} %bitcast.12, s32[1,2048]{1,0:T(1,128)S(1)} %bitcast.13, bf16[8,16]{1,0:T(8,128)(2,1)S(1)} %bitcast.15, ...), custom_call_target="tpu_custom_call" | custom-call | tf_op jit(solution)/shard_map/pallas_call | solution.py:343
  22.8 0.7 %copy.12 = bf16[512,128]{1,0:T(8,128)(2,1)} copy(bf16[512,128]{1,0:T(8,128)(2,1)S(1)} %get-tuple-element.4) | data formatting | bytes 262144
  23.4 0.6 %copy.13 = f32[8,1024]{1,0:T(8,128)} copy(f32[8,1024]{1,0:T(8,128)S(1)} %get-tuple-element.5) | data formatting | bytes 65536
Async XLA Ops:
  0.6 0.7 %copy-start.1 = (bf16[2048,2]{0,1:T(2,128)(2,1)S(1)}, bf16[2048,2]{0,1:T(2,128)(2,1)}, u32[]{:S(2)}) copy-start(bf16[2048,2]{0,1:T(2,128)(2,1)} %param.9) | copy-start | bytes 24580
  0.6 0.7 %copy-start.4 = (bf16[1024,2]{0,1:T(2,128)(2,1)S(1)}, bf16[1024,2]{0,1:T(2,128)(2,1)}, u32[]{:S(2)}) copy-start(bf16[1024,2]{0,1:T(2,128)(2,1)} %param.13) | copy-start | bytes 12292
  1.3 0.9 %copy-start = (bf16[16,4096]{1,0:T(8,128)(2,1)S(1)}, bf16[16,4096]{1,0:T(8,128)(2,1)}, u32[]{:S(2)}) copy-start(bf16[16,4096]{1,0:T(8,128)(2,1)} %raw_ref.1) | copy-start | bytes 393220
  2.2 0.7 %copy-start.2 = (s32[2048]{0:T(1024)S(1)}, s32[2048]{0:T(1024)}, u32[]{:S(2)}) copy-start(s32[2048]{0:T(1024)} %param.10) | copy-start | bytes 24580
  2.9 0.7 %copy-start.3 = (s32[2048]{0:T(1024)S(1)}, s32[2048]{0:T(1024)}, u32[]{:S(2)}) copy-start(s32[2048]{0:T(1024)} %param.11) | copy-start | bytes 24580
  3.6 0.7 %copy-start.5 = (bf16[16,8]{0,1:T(8,128)(2,1)S(1)}, bf16[16,8]{0,1:T(8,128)(2,1)}, u32[]{:S(2)}) copy-start(bf16[16,8]{0,1:T(8,128)(2,1)} %param.12) | copy-start | bytes 772
  4.3 0.7 %copy-start.6 = (s32[1,8,4]{1,2,0:T(4,128)S(1)}, s32[1,8,4]{1,2,0:T(4,128)}, u32[]{:S(2)}) copy-start(s32[1,8,4]{1,2,0:T(4,128)} %param.14) | copy-start | bytes 388
  5.0 0.7 %copy-start.7 = (f32[1,8,4]{1,2,0:T(4,128)S(1)}, f32[1,8,4]{1,2,0:T(4,128)}, u32[]{:S(2)}) copy-start(f32[1,8,4]{1,2,0:T(4,128)} %param.15) | copy-start | bytes 388

commit v2 on v1

--- a/solution.py
+++ b/solution.py
@@ -11,6 +11,7 @@
 PROWS = 16
 LANES = 128
 GROUP = 16
+BATCH = 4
 MESH = pl.DeviceIdType.MESH
 
 
@@ -40,6 +41,16 @@
 def kernel(
     devices,
     across,
+    raw_in,
+    rtaps_in,
+    offset_in,
+    band_in,
+    table_in,
+    ataps_in,
+    list_in,
+    frac_in,
+    focused_ref,
+    tiles_ref,
     raw_ref,
     rtaps_ref,
     offset_ref,
@@ -48,8 +59,6 @@
     ataps_ref,
     list_ref,
     frac_ref,
-    focused_ref,
-    tiles_ref,
     zr_ref,
     zi_ref,
     zn_ref,
@@ -60,11 +69,13 @@
     b_ref,
     send_ref,
     recv_ref,
+    focus_ref,
     power_ref,
     low_ref,
     high_ref,
     from_next_ref,
     from_prev_ref,
+    in_sems,
     send_sem,
     recv_sem,
     low_send_sem,
@@ -82,6 +93,26 @@
     rwidth = zr_ref.shape[1]
     awidth = za_ref.shape[1]
 
+    rtaps_copy, offset_copy, band_copy, table_copy, raw_copy, ataps_copy, list_copy, frac_copy = [
+        pltpu.make_async_copy(outside, inside, in_sems.at[at])
+        for at, (outside, inside) in enumerate(
+            (
+                (rtaps_in, rtaps_ref),
+                (offset_in, offset_ref),
+                (band_in, band_ref),
+                (table_in, table_ref),
+                (raw_in, raw_ref),
+                (ataps_in, ataps_ref),
+                (list_in, list_ref),
+                (frac_in, frac_ref),
+            )
+        )
+    ]
+    first_copies = (rtaps_copy, offset_copy, band_copy, table_copy, raw_copy)
+    later_copies = (ataps_copy, list_copy, frac_copy)
+    for copy in first_copies + later_copies:
+        copy.start()
+
     def place(index):
         return (lax.div(index, across), lax.rem(index, across))
 
@@ -99,6 +130,15 @@
             body(0)
         else:
             lax.fori_loop(0, groups, lambda g, c: (body(g * GROUP), c)[1], 0)
+
+    for copy in first_copies:
+        copy.wait()
+
+    for step, real_rows in shifted_rows(rtaps_ref[0:1, :], rwidth):
+        zr_ref[16 * step : 16 * step + 16, :] = real_rows.astype(jnp.bfloat16)
+    for step, imag_rows in shifted_rows(rtaps_ref[1:2, :], rwidth):
+        zi_ref[16 * step : 16 * step + 16, :] = imag_rows.astype(jnp.bfloat16)
+        zn_ref[16 * step : 16 * step + 16, :] = (-imag_rows).astype(jnp.bfloat16)
 
     side = (2 * LANES, 2 * LANES)
     column = iota(side, 1)
@@ -113,12 +153,6 @@
     spare = x_ref.shape[0] - chunks * rows
     if spare:
         x_ref[chunks * rows :, :] = jnp.zeros((spare, 2 * LANES), jnp.bfloat16)
-
-    for step, real_rows in shifted_rows(rtaps_ref[0:1, :], rwidth):
-        zr_ref[16 * step : 16 * step + 16, :] = real_rows.astype(jnp.bfloat16)
-    for step, imag_rows in shifted_rows(rtaps_ref[1:2, :], rwidth):
-        zi_ref[16 * step : 16 * step + 16, :] = imag_rows.astype(jnp.bfloat16)
-        zn_ref[16 * step : 16 * step + 16, :] = (-imag_rows).astype(jnp.bfloat16)
 
     def range_group(first):
         for apart in range(rwidth // LANES):
@@ -158,8 +192,9 @@
     left = iota((rows, LANES), 1) < LANES // 2
 
     def migrate_group(first):
-        for j in range(GROUP):
-            at = pl.multiple_of((first + j) * LANES, LANES)
+        chunk_at = [lax.rem(lax.div(me, 2) + first + 1 + j, chunks) for j in range(GROUP)]
+        for j, chunk in enumerate(chunk_at):
+            at = pl.multiple_of(chunk * LANES, LANES)
             offsets = offset_ref[:, pl.ds(at, LANES)]
             chosen = band_ref[:, pl.ds(at, LANES)]
             onehot = (iota((bands, LANES), 0) == chosen).astype(jnp.float32).astype(jnp.bfloat16)
@@ -168,8 +203,9 @@
             for tap in range(taps):
                 banded = jnp.where(delta == offsets + tap, weights[tap : tap + 1, :], banded)
             b_ref[j] = banded.astype(jnp.bfloat16)
-        for j in range(GROUP):
-            start = pl.multiple_of((first + j) * rows, 16)
+
+        for j, chunk in enumerate(chunk_at):
+            start = pl.multiple_of(chunk * rows, 16)
             before = f_ref[pl.ds(start, rows), :]
             here = f_ref[pl.ds(pl.multiple_of(start + rows, 16), rows), :]
             after = f_ref[pl.ds(pl.multiple_of(start + 2 * rows, 16), rows), :]
@@ -183,28 +219,39 @@
             real_part, imag_part = moved[:rows], moved[rows:]
             even = jnp.where(left, real_part, pltpu.roll(imag_part, LANES // 2, 1))
             odd = jnp.where(left, pltpu.roll(real_part, LANES // 2, 1), imag_part)
-            send_ref[2 * (first + j)] = even.astype(jnp.bfloat16)
-            send_ref[2 * (first + j) + 1] = odd.astype(jnp.bfloat16)
-
+            send_ref[2 * chunk] = even.astype(jnp.bfloat16)
+            send_ref[2 * chunk + 1] = odd.astype(jnp.bfloat16)
+            if j % BATCH == BATCH - 1:
+                if groups == 1 and j == BATCH - 1:
+                    pl.semaphore_wait(barrier, devices - 1)
+                for ready in range(j + 1 - BATCH, j + 1):
+                    for half in range(2):
+                        own_possible = groups > 1 or ready == GROUP - 1
+                        send(2 * chunk_at[ready] + half, own_possible)
+
+    def send(other, own_possible):
+        def go():
+            pltpu.make_async_remote_copy(
+                src_ref=send_ref.at[other],
+                dst_ref=recv_ref.at[me],
+                send_sem=send_sem,
+                recv_sem=recv_sem,
+                device_id=place(other),
+                device_id_type=MESH,
+            ).start()
+
+        if own_possible:
+            pl.when(other != me)(go)
+        else:
+            go()
+
+    if groups > 1:
+        pl.semaphore_wait(barrier, devices - 1)
     each_group(migrate_group)
-
-    pl.semaphore_wait(barrier, devices - 1)
-
-    def send(distance, carry):
-        other = lax.rem(me + distance, devices)
-        pltpu.make_async_remote_copy(
-            src_ref=send_ref.at[other],
-            dst_ref=recv_ref.at[me],
-            send_sem=send_sem,
-            recv_sem=recv_sem,
-            device_id=place(other),
-            device_id_type=MESH,
-        ).start()
-        return carry
-
-    lax.fori_loop(1, devices, send, 0)
     recv_ref[me] = send_ref[me]
 
+    for copy in later_copies:
+        copy.wait()
     for step, real_rows in shifted_rows(ataps_ref[0:1, :], awidth):
         za_ref[16 * step : 16 * step + 16, :] = real_rows.astype(jnp.bfloat16)
     for step, imag_rows in shifted_rows(ataps_ref[1:2, :], awidth):
@@ -234,9 +281,7 @@
         product = jnp.dot(za_ref[:, :depth], columns, preferred_element_type=jnp.float32)
         focus = product[:LANES] + sign * pltpu.roll(product[LANES:], LANES // 2, 1)
         at = slice(LANES * block, LANES * (block + 1))
-        focused_ref[at, :] = jnp.dot(
-            focus.astype(jnp.bfloat16), parts_beside, preferred_element_type=jnp.float32
-        ).astype(jnp.bfloat16)
+        focus_ref[at, :] = focus.astype(jnp.bfloat16)
         power_ref[at, :] = focus * focus
 
     stride = LOOKS * PROWS
@@ -252,11 +297,16 @@
             summed.append(total + pltpu.roll(total, LANES // 2, 1))
         pieces.append(jnp.where(left_half, summed[0], summed[1]) * (1.0 / LOOKS))
     looked = jnp.concatenate(pieces, 1)
-    partial = jnp.dot(
-        spread, looked, precision=lax.Precision.HIGHEST, preferred_element_type=jnp.float32
-    )
-    low_ref[...] = partial[:patches]
-    high_ref[...] = partial[2 * patches :]
+
+    def tile_sums(first):
+        weights = spread[first : first + patches]
+        total = weights[:, 0:1] * looked[0:1, :]
+        for patch in range(1, patches):
+            total += weights[:, patch : patch + 1] * looked[patch : patch + 1, :]
+        return total
+
+    low_ref[...] = tile_sums(0)
+    high_ref[...] = tile_sums(2 * patches)
 
     def low_copy():
         return pltpu.make_async_remote_copy(
@@ -286,7 +336,10 @@
     def _():
         high_copy().start()
 
-    tiles_ref[...] = partial[patches : 2 * patches]
+    tiles_ref[...] = tile_sums(patches)
+    focused_ref[...] = jnp.dot(
+        focus_ref[...], parts_beside, preferred_element_type=jnp.float32
+    ).astype(jnp.bfloat16)
     pltpu.make_async_copy(send_ref.at[others], send_ref.at[others], send_sem).wait()
 
     @pl.when(me < devices - 1)
@@ -306,6 +359,17 @@
     @pl.when(me < devices - 1)
     def _():
         high_copy().wait_send()
+
+
+def hand_out(focused_ref, tiles_ref, focused_out, tiles_out, sems):
+    copies = (
+        pltpu.make_async_copy(focused_ref, focused_out, sems.at[0]),
+        pltpu.make_async_copy(tiles_ref, tiles_out, sems.at[1]),
+    )
+    for copy in copies:
+        copy.start()
+    for copy in copies:
+        copy.wait()
 
 
 def body(
@@ -323,7 +387,17 @@
     awidth = min(pulses, azimuth_taps.shape[0] + LANES)
     spare = 0 if chunks == GROUP else rwidth // LANES
     whole = pl.BlockSpec(memory_space=pltpu.VMEM)
-    scratch = [
+    operands = (
+        raw_echoes,
+        range_taps.T,
+        mig_offset.reshape(1, bins),
+        interp_band.reshape(1, bins),
+        interp_table.T,
+        azimuth_taps.T,
+        geo_list[0].T,
+        geo_frac[0].T,
+    )
+    scratch = [pltpu.VMEM(operand.shape, operand.dtype) for operand in operands] + [
         pltpu.VMEM((LANES, rwidth), jnp.bfloat16),
         pltpu.VMEM((LANES, rwidth), jnp.bfloat16),
         pltpu.VMEM((LANES, rwidth), jnp.bfloat16),
@@ -334,34 +408,35 @@
         pltpu.VMEM((GROUP, 2 * LANES, LANES), jnp.bfloat16),
         pltpu.VMEM((devices, rows, LANES), jnp.bfloat16),
         pltpu.VMEM((devices, rows, LANES), jnp.bfloat16),
+        pltpu.VMEM((pulses, LANES), jnp.bfloat16),
         pltpu.VMEM((pulses, LANES), jnp.float32),
         pltpu.VMEM((patches, tile), jnp.float32),
         pltpu.VMEM((patches, tile), jnp.float32),
         pltpu.VMEM((patches, tile), jnp.float32),
         pltpu.VMEM((patches, tile), jnp.float32),
-    ] + [pltpu.SemaphoreType.DMA] * 6
-    return pl.pallas_call(
+    ] + [pltpu.SemaphoreType.DMA((8,))] + [pltpu.SemaphoreType.DMA] * 6
+    shapes = (
+        jax.ShapeDtypeStruct((pulses, breadth // devices), jnp.bfloat16),
+        jax.ShapeDtypeStruct((patches, tile), jnp.float32),
+    )
+    outside = pl.BlockSpec(memory_space=pltpu.HBM)
+    results = pl.pallas_call(
         functools.partial(kernel, devices, across),
-        out_shape=(
-            jax.ShapeDtypeStruct((pulses, breadth // devices), jnp.bfloat16),
-            jax.ShapeDtypeStruct((patches, tile), jnp.float32),
-        ),
-        in_specs=[whole] * 8,
+        out_shape=shapes,
+        in_specs=[outside] * 8,
         out_specs=(whole, whole),
         scratch_shapes=scratch,
         compiler_params=pltpu.CompilerParams(
             collective_id=0, has_side_effects=True, vmem_limit_bytes=40 * 2**20
         ),
-    )(
-        raw_echoes,
-        range_taps.T,
-        mig_offset.reshape(1, bins),
-        interp_band.reshape(1, bins),
-        interp_table.T,
-        azimuth_taps.T,
-        geo_list[0].T,
-        geo_frac[0].T,
-    )
+    )(*[pltpu.with_memory_space_constraint(operand, pltpu.HBM) for operand in operands])
+    return pl.pallas_call(
+        hand_out,
+        out_shape=shapes,
+        in_specs=[whole] * 2,
+        out_specs=(outside, outside),
+        scratch_shapes=[pltpu.SemaphoreType.DMA((2,))],
+    )(*results)
 
 
 def solution(mesh):

time: 24.4 us -> 21.1 us (0.86)
  local copies, waits for them, and re-layouts: 6.3 us -> 1.25 us
  Pallas kernels: 17.1 us -> 19 us
    unnamed x18 -> x4, local copies, waits for them, and re-layouts: 6.3 us -> 1.25 us
    pallas_call x1 -> x2, Pallas kernels: 17.1 us -> 19 us  [the longest x1 17.4 us: body(): pl.pallas_call(functools.partial(kernel, devices, across), out_shape=shap...]
where the time goes in v2:
time: 21.1 us; the launch traced here: 20.9 us
  Pallas kernels  19 us (90%)
  local copies, waits for them, and re-layouts  1.25 us (6%)
  between operations  0.65 us (3%)
    pallas_call x1, Pallas kernels, body(): pl.pallas_call(functools.partial(kernel, devices, across), out_shape=shap...  17.4 us
    pallas_call x1, Pallas kernels, body(): pl.pallas_call(hand_out, out_shape=shapes, in_specs=[whole] * 2, out_spec...  1.58 us
    unnamed x4, local copies, waits for them, and re-layouts  1.25 us

profile of v2, /device:TPU:1, one launch (start us, length us, event | category | flops | bytes accessed | tf_op | source)
XLA Modules:
  0.0 20.9 jit_solution(7953392957143245879)
XLA Ops:
  0.6 17.4 %shard_map.95 = (bf16[512,128]{1,0:T(8,128)(2,1)S(1)}, f32[8,1024]{1,0:T(8,128)S(1)}) custom-call(bf16[16,4096]{1,0:T(8,128)(2,1)} %raw_in.1, bf16[2,2048]{1,0:T(2,128)(2,1)} %bitcast.11, s32[1,2048]{1,0:T(1,128)} %bitcast.12, s32[1,2048]{1,0:T(1,128)} %bitcast.13, bf16[8,16]{1,0:T(8,128)(2,1)} %bitcast.15, bf16[2,1024]{1,0:T(2,128)(2,1)} %bitcast.14, ...), custom_call_target="tpu_custom_call" | custom-call | tf_op jit(solution)/shard_map/pallas_call | solution.py:423
  18.0 0.0 copy-start
  18.0 0.6 %copy-done = bf16[512,128]{1,0:T(8,128)(2,1)} copy-done((bf16[512,128]{1,0:T(8,128)(2,1)}, bf16[512,128]{1,0:T(8,128)(2,1)S(1)}, u32[]{:S(2)}) %copy-start) | copy-done | bytes 131096
  18.7 0.0 copy-start.1
  18.7 0.6 %copy-done.1 = f32[8,1024]{1,0:T(8,128)} copy-done((f32[8,1024]{1,0:T(8,128)}, f32[8,1024]{1,0:T(8,128)S(1)}, u32[]{:S(2)}) %copy-start.1) | copy-done | bytes 32792
  19.3 1.6 %shard_map.96 = (bf16[512,128]{1,0:T(8,128)(2,1)}, f32[8,1024]{1,0:T(8,128)}) custom-call(bf16[512,128]{1,0:T(8,128)(2,1)} %copy-done, f32[8,1024]{1,0:T(8,128)} %copy-done.1), custom_call_target="tpu_custom_call" | custom-call | tf_op jit(solution)/shard_map/pallas_call | solution.py:433
Async XLA Ops:
  18.0 0.6 %copy-start = (bf16[512,128]{1,0:T(8,128)(2,1)}, bf16[512,128]{1,0:T(8,128)(2,1)S(1)}, u32[]{:S(2)}) copy-start(bf16[512,128]{1,0:T(8,128)(2,1)S(1)} %get-tuple-element.4.focused_ref) | copy-start | bytes 393220
  18.7 0.6 %copy-start.1 = (f32[8,1024]{1,0:T(8,128)}, f32[8,1024]{1,0:T(8,128)S(1)}, u32[]{:S(2)}) copy-start(f32[8,1024]{1,0:T(8,128)S(1)} %get-tuple-element.5.tiles_ref) | copy-start | bytes 98308

commit v3 on v2

--- a/solution.py
+++ b/solution.py
@@ -66,6 +66,7 @@
     x_ref,
     sum_ref,
     f_ref,
+    kernel_ref,
     b_ref,
     send_ref,
     recv_ref,
@@ -131,14 +132,16 @@
         else:
             lax.fori_loop(0, groups, lambda g, c: (body(g * GROUP), c)[1], 0)
 
-    for copy in first_copies:
-        copy.wait()
+    rtaps_copy.wait()
 
     for step, real_rows in shifted_rows(rtaps_ref[0:1, :], rwidth):
         zr_ref[16 * step : 16 * step + 16, :] = real_rows.astype(jnp.bfloat16)
     for step, imag_rows in shifted_rows(rtaps_ref[1:2, :], rwidth):
         zi_ref[16 * step : 16 * step + 16, :] = imag_rows.astype(jnp.bfloat16)
         zn_ref[16 * step : 16 * step + 16, :] = (-imag_rows).astype(jnp.bfloat16)
+
+    for copy in first_copies[1:]:
+        copy.wait()
 
     side = (2 * LANES, 2 * LANES)
     column = iota(side, 1)
@@ -154,9 +157,32 @@
     if spare:
         x_ref[chunks * rows :, :] = jnp.zeros((spare, 2 * LANES), jnp.bfloat16)
 
+    bands, bins = table_ref.shape[1], chunks * LANES
+    onehot = (iota((bands, bins), 0) == band_ref[...]).astype(jnp.float32).astype(jnp.bfloat16)
+    kernel_ref[...] = jnp.dot(table_ref[...], onehot, preferred_element_type=jnp.float32)
+    window = (2 * LANES, LANES)
+    lane = iota(window, 0) % LANES
+    shift = jnp.where(lane < LANES // 2, -LANES, LANES)
+    bin_of = LANES - 1 - lane + jnp.where(iota(window, 0) < LANES, 0, shift)
+    delta = (bin_of - iota(window, 1) + 3).astype(jnp.int16)
+
+    def band_matrix(chunk):
+        at = pl.ds(pl.multiple_of(chunk * LANES, LANES), LANES)
+        offsets = jnp.broadcast_to(offset_ref[:, at], (16, LANES)).astype(jnp.int16)
+        distance = delta - jnp.broadcast_to(offsets[0:1], window)
+        weights = kernel_ref[:, at]
+        banded = jnp.zeros(window, jnp.bfloat16)
+        for tap in range(weights.shape[0]):
+            weight = jnp.broadcast_to(weights[tap : tap + 1], (16, LANES)).astype(jnp.bfloat16)
+            weight = jnp.broadcast_to(weight[0:1], window)
+            banded = jnp.where(distance == jnp.int16(tap), weight, banded)
+        b_ref[chunk] = banded
+
     def range_group(first):
         for apart in range(rwidth // LANES):
             count = GROUP - apart if groups == 1 else GROUP
+            if apart < GROUP:
+                band_matrix(first + apart)
             if count <= 0:
                 continue
             at = slice(LANES * apart, LANES * (apart + 1))
@@ -181,29 +207,11 @@
     f_ref[(chunks + 1) * rows :, :] = jnp.zeros((rows, 2 * LANES), jnp.bfloat16)
     each_group(range_group)
 
-    window = (2 * LANES, LANES)
-    lane = iota(window, 0) % LANES
-    shift = jnp.where(lane < LANES // 2, -LANES, LANES)
-    bin_of = LANES - 1 - lane + jnp.where(iota(window, 0) < LANES, 0, shift)
-    delta = bin_of - iota(window, 1) + 3
-    taps = table_ref.shape[0]
-    bands = table_ref.shape[1]
-    table = table_ref[...]
     left = iota((rows, LANES), 1) < LANES // 2
 
     def migrate_group(first):
-        chunk_at = [lax.rem(lax.div(me, 2) + first + 1 + j, chunks) for j in range(GROUP)]
-        for j, chunk in enumerate(chunk_at):
-            at = pl.multiple_of(chunk * LANES, LANES)
-            offsets = offset_ref[:, pl.ds(at, LANES)]
-            chosen = band_ref[:, pl.ds(at, LANES)]
-            onehot = (iota((bands, LANES), 0) == chosen).astype(jnp.float32).astype(jnp.bfloat16)
-            weights = jnp.dot(table, onehot, preferred_element_type=jnp.float32)
-            banded = jnp.zeros(window, jnp.float32)
-            for tap in range(taps):
-                banded = jnp.where(delta == offsets + tap, weights[tap : tap + 1, :], banded)
-            b_ref[j] = banded.astype(jnp.bfloat16)
-
+        ahead = list(range(1, GROUP, 2)) + list(range(2, GROUP + 1, 2))
+        chunk_at = [lax.rem(lax.div(me, 2) + first + step, chunks) for step in ahead]
         for j, chunk in enumerate(chunk_at):
             start = pl.multiple_of(chunk * rows, 16)
             before = f_ref[pl.ds(start, rows), :]
@@ -214,7 +222,7 @@
                 around = jnp.where(left, before[:, part], after[:, part])
                 both.append(jnp.concatenate([here[:, part], around], 1))
             moved = jnp.dot(
-                jnp.concatenate(both, 0), b_ref[j], preferred_element_type=jnp.float32
+                jnp.concatenate(both, 0), b_ref[chunk], preferred_element_type=jnp.float32
             )
             real_part, imag_part = moved[:rows], moved[rows:]
             even = jnp.where(left, real_part, pltpu.roll(imag_part, LANES // 2, 1))
@@ -359,17 +367,6 @@
     @pl.when(me < devices - 1)
     def _():
         high_copy().wait_send()
-
-
-def hand_out(focused_ref, tiles_ref, focused_out, tiles_out, sems):
-    copies = (
-        pltpu.make_async_copy(focused_ref, focused_out, sems.at[0]),
-        pltpu.make_async_copy(tiles_ref, tiles_out, sems.at[1]),
-    )
-    for copy in copies:
-        copy.start()
-    for copy in copies:
-        copy.wait()
 
 
 def body(
@@ -405,7 +402,8 @@
         pltpu.VMEM(((chunks + spare) * rows, 2 * LANES), jnp.bfloat16),
         pltpu.VMEM((GROUP * rows, 2 * LANES), jnp.float32),
         pltpu.VMEM(((chunks + 2) * rows, 2 * LANES), jnp.bfloat16),
-        pltpu.VMEM((GROUP, 2 * LANES, LANES), jnp.bfloat16),
+        pltpu.VMEM((interp_table.shape[1], bins), jnp.float32),
+        pltpu.VMEM((chunks, 2 * LANES, LANES), jnp.bfloat16),
         pltpu.VMEM((devices, rows, LANES), jnp.bfloat16),
         pltpu.VMEM((devices, rows, LANES), jnp.bfloat16),
         pltpu.VMEM((pulses, LANES), jnp.bfloat16),
@@ -420,7 +418,7 @@
         jax.ShapeDtypeStruct((patches, tile), jnp.float32),
     )
     outside = pl.BlockSpec(memory_space=pltpu.HBM)
-    results = pl.pallas_call(
+    return pl.pallas_call(
         functools.partial(kernel, devices, across),
         out_shape=shapes,
         in_specs=[outside] * 8,
@@ -430,13 +428,6 @@
             collective_id=0, has_side_effects=True, vmem_limit_bytes=40 * 2**20
         ),
     )(*[pltpu.with_memory_space_constraint(operand, pltpu.HBM) for operand in operands])
-    return pl.pallas_call(
-        hand_out,
-        out_shape=shapes,
-        in_specs=[whole] * 2,
-        out_specs=(outside, outside),
-        scratch_shapes=[pltpu.SemaphoreType.DMA((2,))],
-    )(*results)
 
 
 def solution(mesh):

time: 21.1 us -> 18.7 us (0.89)
  Pallas kernels: 19 us -> 16.6 us
    pallas_call x1 -> x0, Pallas kernels: 1.58 us -> none  [body(): pl.pallas_call(hand_out, out_shape=shapes, in_specs=[whole] * 2, out_spec...]
    pallas_call x1, Pallas kernels: 17.4 us -> 16.6 us  [body(): pl.pallas_call(functools.partial(kernel, devices, across), out_shape=shap...]
    unnamed x4 -> x2, local copies, waits for them, and re-layouts: 1.25 us -> 1.27 us
where the time goes in v3:
time: 18.7 us; the launch traced here: 18.5 us
  Pallas kernels  16.6 us (89%)
  local copies, waits for them, and re-layouts  1.27 us (7%)
  between operations  0.64 us (3%)
    pallas_call x1, Pallas kernels, body(): pl.pallas_call(functools.partial(kernel, devices, across), out_shape=shap...  16.6 us
    unnamed x2, local copies, waits for them, and re-layouts  1.27 us

profile of v3, /device:TPU:1, one launch (start us, length us, event | category | flops | bytes accessed | tf_op | source)
XLA Modules:
  0.0 18.5 jit_solution(3061116565809433103)
XLA Ops:
  0.6 16.6 %shard_map.95 = (bf16[512,128]{1,0:T(8,128)(2,1)S(1)}, f32[8,1024]{1,0:T(8,128)S(1)}) custom-call(bf16[16,4096]{1,0:T(8,128)(2,1)} %raw_in.1, bf16[2,2048]{1,0:T(2,128)(2,1)} %bitcast.11, s32[1,2048]{1,0:T(1,128)} %bitcast.12, s32[1,2048]{1,0:T(1,128)} %bitcast.13, bf16[8,16]{1,0:T(8,128)(2,1)} %bitcast.15, bf16[2,1024]{1,0:T(2,128)(2,1)} %bitcast.14, ...), custom_call_target="tpu_custom_call" | custom-call | tf_op jit(solution)/shard_map/pallas_call | solution.py:421
  17.2 0.7 %copy.12 = bf16[512,128]{1,0:T(8,128)(2,1)} copy(bf16[512,128]{1,0:T(8,128)(2,1)S(1)} %get-tuple-element.4) | data formatting | bytes 262144
  17.8 0.6 %copy.13 = f32[8,1024]{1,0:T(8,128)} copy(f32[8,1024]{1,0:T(8,128)S(1)} %get-tuple-element.5) | data formatting | bytes 65536

commit v4 on v3

--- a/solution.py
+++ b/solution.py
@@ -28,14 +28,13 @@
     row = iota((8, width), 0)
     for bit in (1, 2, 4):
         eight = jnp.where((row & bit) != 0, pltpu.roll(eight, bit, 1), eight)
-    for step in range(LANES // 16):
-        halves = []
-        for start in (16 * step, 16 * step + 8):
-            moved = eight if start == 0 else pltpu.roll(eight, start, 1)
-            keep = iota((8, LANES), 1) >= iota((8, LANES), 0) + start
-            first = jnp.where(keep, moved[:, :LANES], 0.0)
-            halves.append(jnp.concatenate([first, moved[:, LANES:]], 1))
-        yield step, jnp.concatenate(halves, 0)
+    both = jnp.concatenate([eight, pltpu.roll(eight, 8, 1)], 0).astype(jnp.bfloat16)
+    tile = (16, LANES)
+    for start in range(0, LANES, 16):
+        moved = both if start == 0 else pltpu.roll(both, start, 1)
+        keep = iota(tile, 1) >= iota(tile, 0) + start
+        first = jnp.where(keep, moved[:, :LANES], jnp.zeros(tile, jnp.bfloat16))
+        yield start, jnp.concatenate([first, moved[:, LANES:]], 1)
 
 
 def kernel(
@@ -94,15 +93,15 @@
     rwidth = zr_ref.shape[1]
     awidth = za_ref.shape[1]
 
-    rtaps_copy, offset_copy, band_copy, table_copy, raw_copy, ataps_copy, list_copy, frac_copy = [
+    rtaps_copy, raw_copy, offset_copy, band_copy, table_copy, ataps_copy, list_copy, frac_copy = [
         pltpu.make_async_copy(outside, inside, in_sems.at[at])
         for at, (outside, inside) in enumerate(
             (
                 (rtaps_in, rtaps_ref),
+                (raw_in, raw_ref),
                 (offset_in, offset_ref),
                 (band_in, band_ref),
                 (table_in, table_ref),
-                (raw_in, raw_ref),
                 (ataps_in, ataps_ref),
                 (list_in, list_ref),
                 (frac_in, frac_ref),
@@ -124,7 +123,11 @@
         pl.semaphore_signal(barrier, inc=1, device_id=place(other), device_id_type=MESH)
         return carry
 
-    lax.fori_loop(1, devices, greet, 0)
+    if groups == 1:
+        for distance in range(1, devices):
+            greet(distance, 0)
+    else:
+        lax.fori_loop(1, devices, greet, 0)
 
     def each_group(body):
         if groups == 1:
@@ -134,11 +137,11 @@
 
     rtaps_copy.wait()
 
-    for step, real_rows in shifted_rows(rtaps_ref[0:1, :], rwidth):
-        zr_ref[16 * step : 16 * step + 16, :] = real_rows.astype(jnp.bfloat16)
-    for step, imag_rows in shifted_rows(rtaps_ref[1:2, :], rwidth):
-        zi_ref[16 * step : 16 * step + 16, :] = imag_rows.astype(jnp.bfloat16)
-        zn_ref[16 * step : 16 * step + 16, :] = (-imag_rows).astype(jnp.bfloat16)
+    for start, real_rows in shifted_rows(rtaps_ref[0:1, :], rwidth):
+        zr_ref[start : start + 16, :] = real_rows
+    for start, imag_rows in shifted_rows(rtaps_ref[1:2, :], rwidth):
+        zi_ref[start : start + 16, :] = imag_rows
+        zn_ref[start : start + 16, :] = -imag_rows
 
     for copy in first_copies[1:]:
         copy.wait()
@@ -212,7 +215,8 @@
     def migrate_group(first):
         ahead = list(range(1, GROUP, 2)) + list(range(2, GROUP + 1, 2))
         chunk_at = [lax.rem(lax.div(me, 2) + first + step, chunks) for step in ahead]
-        for j, chunk in enumerate(chunk_at):
+
+        def migrated(chunk):
             start = pl.multiple_of(chunk * rows, 16)
             before = f_ref[pl.ds(start, rows), :]
             here = f_ref[pl.ds(pl.multiple_of(start + rows, 16), rows), :]
@@ -227,15 +231,21 @@
             real_part, imag_part = moved[:rows], moved[rows:]
             even = jnp.where(left, real_part, pltpu.roll(imag_part, LANES // 2, 1))
             odd = jnp.where(left, pltpu.roll(real_part, LANES // 2, 1), imag_part)
-            send_ref[2 * chunk] = even.astype(jnp.bfloat16)
-            send_ref[2 * chunk + 1] = odd.astype(jnp.bfloat16)
-            if j % BATCH == BATCH - 1:
-                if groups == 1 and j == BATCH - 1:
-                    pl.semaphore_wait(barrier, devices - 1)
-                for ready in range(j + 1 - BATCH, j + 1):
-                    for half in range(2):
-                        own_possible = groups > 1 or ready == GROUP - 1
-                        send(2 * chunk_at[ready] + half, own_possible)
+            return even.astype(jnp.bfloat16), odd.astype(jnp.bfloat16)
+
+        later = [migrated(chunk) for chunk in chunk_at[:BATCH]]
+        for at in range(0, GROUP, BATCH):
+            now = later
+            later = [migrated(chunk) for chunk in chunk_at[at + BATCH : at + 2 * BATCH]]
+            batch = list(enumerate(chunk_at))[at : at + BATCH]
+            for (j, chunk), pair in zip(batch, now):
+                for half in range(2):
+                    send_ref[2 * chunk + half] = pair[half]
+            if groups == 1 and at == 0:
+                pl.semaphore_wait(barrier, devices - 1)
+            for j, chunk in batch:
+                for half in range(2):
+                    send(2 * chunk + half, groups > 1 or j == GROUP - 1)
 
     def send(other, own_possible):
         def go():
@@ -260,10 +270,10 @@
 
     for copy in later_copies:
         copy.wait()
-    for step, real_rows in shifted_rows(ataps_ref[0:1, :], awidth):
-        za_ref[16 * step : 16 * step + 16, :] = real_rows.astype(jnp.bfloat16)
-    for step, imag_rows in shifted_rows(ataps_ref[1:2, :], awidth):
-        za_ref[LANES + 16 * step : LANES + 16 * step + 16, :] = imag_rows.astype(jnp.bfloat16)
+    for part in range(2):
+        for start, moved_rows in shifted_rows(ataps_ref[part : part + 1, :], awidth):
+            at = LANES * part + start
+            za_ref[at : at + 16, :] = moved_rows
 
     base = (me - 1) * patches
     slot = iota((3 * patches, patches), 0) + base

time: 18.7 us -> 18.6 us (level)
  Pallas kernels: 16.6 us -> 16.4 us
where the time goes in v4:
time: 18.6 us; the launch traced here: 18.3 us
  Pallas kernels  16.4 us (88%)
  local copies, waits for them, and re-layouts  1.27 us (7%)
  between operations  0.64 us (3%)
    pallas_call x1, Pallas kernels, body(): pl.pallas_call(functools.partial(kernel, devices, across), out_shape=shap...  16.4 us
    unnamed x2, local copies, waits for them, and re-layouts  1.27 us

profile of v4, /device:TPU:1, one launch (start us, length us, event | category | flops | bytes accessed | tf_op | source)
XLA Modules:
  0.0 18.3 jit_solution(17822226635638184658)
XLA Ops:
  0.6 16.4 %shard_map.95 = (bf16[512,128]{1,0:T(8,128)(2,1)S(1)}, f32[8,1024]{1,0:T(8,128)S(1)}) custom-call(bf16[16,4096]{1,0:T(8,128)(2,1)} %raw_in.1, bf16[2,2048]{1,0:T(2,128)(2,1)} %bitcast.11, s32[1,2048]{1,0:T(1,128)} %bitcast.12, s32[1,2048]{1,0:T(1,128)} %bitcast.13, bf16[8,16]{1,0:T(8,128)(2,1)} %bitcast.15, bf16[2,1024]{1,0:T(2,128)(2,1)} %bitcast.14, ...), custom_call_target="tpu_custom_call" | custom-call | tf_op jit(solution)/shard_map/pallas_call | solution.py:431
  17.1 0.7 %copy.12 = bf16[512,128]{1,0:T(8,128)(2,1)} copy(bf16[512,128]{1,0:T(8,128)(2,1)S(1)} %get-tuple-element.4) | data formatting | bytes 262144
  17.7 0.6 %copy.13 = f32[8,1024]{1,0:T(8,128)} copy(f32[8,1024]{1,0:T(8,128)S(1)} %get-tuple-element.5) | data formatting | bytes 65536

commit v5 on v4

--- a/solution.py
+++ b/solution.py
@@ -19,7 +19,7 @@
     return lax.broadcasted_iota(jnp.int32, shape, dim)
 
 
-def shifted_rows(taps, width):
+def shifted_rows(taps, width, stride, step):
     have = min(width, taps.shape[1])
     line = taps[:, :have].astype(jnp.float32)
     if have < width:
@@ -27,14 +27,14 @@
     eight = jnp.broadcast_to(line, (8, width))
     row = iota((8, width), 0)
     for bit in (1, 2, 4):
-        eight = jnp.where((row & bit) != 0, pltpu.roll(eight, bit, 1), eight)
-    both = jnp.concatenate([eight, pltpu.roll(eight, 8, 1)], 0).astype(jnp.bfloat16)
+        eight = jnp.where((row & bit) != 0, pltpu.roll(eight, bit * stride, 1), eight)
+    both = jnp.concatenate([eight, pltpu.roll(eight, 8 * stride, 1)], 0).astype(jnp.bfloat16)
     tile = (16, LANES)
-    for start in range(0, LANES, 16):
-        moved = both if start == 0 else pltpu.roll(both, start, 1)
-        keep = iota(tile, 1) >= iota(tile, 0) + start
+    for part in range(LANES // 16):
+        moved = both if part == 0 else pltpu.roll(both, step * part, 1)
+        keep = iota(tile, 1) >= iota(tile, 0) * stride + step * part
         first = jnp.where(keep, moved[:, :LANES], jnp.zeros(tile, jnp.bfloat16))
-        yield start, jnp.concatenate([first, moved[:, LANES:]], 1)
+        yield 16 * part, jnp.concatenate([first, moved[:, LANES:]], 1)
 
 
 def kernel(
@@ -70,14 +70,15 @@
     send_ref,
     recv_ref,
     focus_ref,
-    power_ref,
+    focus_sum_ref,
+    looked_ref,
     low_ref,
     high_ref,
     from_next_ref,
     from_prev_ref,
     in_sems,
     send_sem,
-    recv_sem,
+    recv_sems,
     low_send_sem,
     high_send_sem,
     low_recv_sem,
@@ -90,6 +91,8 @@
     groups = chunks // GROUP
     pulses = devices * rows
     patches = list_ref.shape[1]
+    sources = LANES // rows
+    blocks = pulses // LANES
     rwidth = zr_ref.shape[1]
     awidth = za_ref.shape[1]
 
@@ -110,8 +113,8 @@
     ]
     first_copies = (rtaps_copy, offset_copy, band_copy, table_copy, raw_copy)
     later_copies = (ataps_copy, list_copy, frac_copy)
-    for copy in first_copies + later_copies:
-        copy.start()
+    rtaps_copy.start()
+    raw_copy.start()
 
     def place(index):
         return (lax.div(index, across), lax.rem(index, across))
@@ -128,6 +131,8 @@
             greet(distance, 0)
     else:
         lax.fori_loop(1, devices, greet, 0)
+    for copy in (offset_copy, band_copy, table_copy) + later_copies:
+        copy.start()
 
     def each_group(body):
         if groups == 1:
@@ -137,9 +142,9 @@
 
     rtaps_copy.wait()
 
-    for start, real_rows in shifted_rows(rtaps_ref[0:1, :], rwidth):
+    for start, real_rows in shifted_rows(rtaps_ref[0:1, :], rwidth, 1, 16):
         zr_ref[start : start + 16, :] = real_rows
-    for start, imag_rows in shifted_rows(rtaps_ref[1:2, :], rwidth):
+    for start, imag_rows in shifted_rows(rtaps_ref[1:2, :], rwidth, 1, 16):
         zi_ref[start : start + 16, :] = imag_rows
         zn_ref[start : start + 16, :] = -imag_rows
 
@@ -172,12 +177,12 @@
     def band_matrix(chunk):
         at = pl.ds(pl.multiple_of(chunk * LANES, LANES), LANES)
         offsets = jnp.broadcast_to(offset_ref[:, at], (16, LANES)).astype(jnp.int16)
-        distance = delta - jnp.broadcast_to(offsets[0:1], window)
+        distance = delta - jnp.concatenate([offsets] * (2 * LANES // 16), 0)
         weights = kernel_ref[:, at]
         banded = jnp.zeros(window, jnp.bfloat16)
         for tap in range(weights.shape[0]):
             weight = jnp.broadcast_to(weights[tap : tap + 1], (16, LANES)).astype(jnp.bfloat16)
-            weight = jnp.broadcast_to(weight[0:1], window)
+            weight = jnp.concatenate([weight] * (2 * LANES // 16), 0)
             banded = jnp.where(distance == jnp.int16(tap), weight, banded)
         b_ref[chunk] = banded
 
@@ -253,7 +258,7 @@
                 src_ref=send_ref.at[other],
                 dst_ref=recv_ref.at[me],
                 send_sem=send_sem,
-                recv_sem=recv_sem,
+                recv_sem=recv_sems.at[lax.div(me, sources)],
                 device_id=place(other),
                 device_id_type=MESH,
             ).start()
@@ -266,12 +271,15 @@
     if groups > 1:
         pl.semaphore_wait(barrier, devices - 1)
     each_group(migrate_group)
-    recv_ref[me] = send_ref[me]
+    own_copy = pltpu.make_async_copy(
+        send_ref.at[me], recv_ref.at[me], recv_sems.at[lax.div(me, sources)]
+    )
+    own_copy.start()
 
     for copy in later_copies:
         copy.wait()
     for part in range(2):
-        for start, moved_rows in shifted_rows(ataps_ref[part : part + 1, :], awidth):
+        for start, moved_rows in shifted_rows(ataps_ref[part : part + 1, :], awidth, 8, 1):
             at = LANES * part + start
             za_ref[at : at + 16, :] = moved_rows
 
@@ -289,31 +297,38 @@
     parts_beside = parts_beside.astype(jnp.float32).astype(jnp.bfloat16)
     sign = jnp.where(iota(square, 1) < LANES // 2, -1.0, 1.0)
 
-    others = pl.ds(0, devices - 1)
-    pltpu.make_async_copy(recv_ref.at[others], recv_ref.at[others], recv_sem).wait()
-
-    for block in range(pulses // LANES):
-        depth = min(awidth, pulses - LANES * block)
-        first = LANES * block // rows
-        columns = recv_ref[first : first + depth // rows].reshape(depth, LANES)
-        product = jnp.dot(za_ref[:, :depth], columns, preferred_element_type=jnp.float32)
+    for block in range(blocks):
+        at = pl.ds(sources * block, sources)
+        pltpu.make_async_copy(recv_ref.at[at], recv_ref.at[at], recv_sems.at[block]).wait()
+        columns = recv_ref[sources * block : sources * (block + 1)].reshape(LANES, LANES)
+        for apart in range(min(block + 1, awidth // LANES)):
+            product = jnp.dot(
+                za_ref[:, LANES * apart : LANES * (apart + 1)],
+                columns,
+                preferred_element_type=jnp.float32,
+            )
+            if apart == 0:
+                focus_sum_ref[block] = product
+            else:
+                focus_sum_ref[block - apart] += product
+
+    left_half = iota((LANES // 8, LANES), 1) < LANES // 2
+    for block in range(blocks):
+        product = focus_sum_ref[block]
         focus = product[:LANES] + sign * pltpu.roll(product[LANES:], LANES // 2, 1)
-        at = slice(LANES * block, LANES * (block + 1))
-        focus_ref[at, :] = focus.astype(jnp.bfloat16)
-        power_ref[at, :] = focus * focus
-
-    stride = LOOKS * PROWS
-    left_half = iota((patches, LANES), 1) < LANES // 2
-    pieces = []
-    for piece in range(stride // (2 * LOOKS)):
+        focus_ref[LANES * block : LANES * (block + 1), :] = focus.astype(jnp.bfloat16)
+        power = (focus * focus).reshape(2, LOOKS, LANES // 8, LANES)
         summed = []
         for half in range(2):
-            start = 2 * LOOKS * piece + LOOKS * half
-            total = power_ref[pl.ds(start, patches, stride=stride), :]
+            total = power[half, 0]
             for look in range(1, LOOKS):
-                total += power_ref[pl.ds(start + look, patches, stride=stride), :]
+                total += power[half, look]
             summed.append(total + pltpu.roll(total, LANES // 2, 1))
-        pieces.append(jnp.where(left_half, summed[0], summed[1]) * (1.0 / LOOKS))
+        looked_ref[LANES // 8 * block : LANES // 8 * (block + 1), :] = jnp.where(
+            left_half, summed[0], summed[1]
+        ) * (1.0 / LOOKS)
+    stride = LOOKS * PROWS // 8
+    pieces = [looked_ref[pl.ds(piece, patches, stride=stride), :] for piece in range(stride)]
     looked = jnp.concatenate(pieces, 1)
 
     def tile_sums(first):
@@ -355,9 +370,16 @@
         high_copy().start()
 
     tiles_ref[...] = tile_sums(patches)
-    focused_ref[...] = jnp.dot(
-        focus_ref[...], parts_beside, preferred_element_type=jnp.float32
-    ).astype(jnp.bfloat16)
+    row = iota(square, 0)
+    in_order = (column == row % 8 * (LANES // 8) + row // 8).astype(jnp.float32)
+    in_order = in_order.astype(jnp.bfloat16)
+    for block in range(blocks):
+        at = slice(LANES * block, LANES * (block + 1))
+        ordered = jnp.dot(in_order, focus_ref[at, :], preferred_element_type=jnp.float32)
+        focused_ref[at, :] = jnp.dot(
+            ordered.astype(jnp.bfloat16), parts_beside, preferred_element_type=jnp.float32
+        ).astype(jnp.bfloat16)
+    others = pl.ds(0, devices - 1)
     pltpu.make_async_copy(send_ref.at[others], send_ref.at[others], send_sem).wait()
 
     @pl.when(me < devices - 1)
@@ -417,12 +439,17 @@
         pltpu.VMEM((devices, rows, LANES), jnp.bfloat16),
         pltpu.VMEM((devices, rows, LANES), jnp.bfloat16),
         pltpu.VMEM((pulses, LANES), jnp.bfloat16),
-        pltpu.VMEM((pulses, LANES), jnp.float32),
+        pltpu.VMEM((pulses // LANES, 2 * LANES, LANES), jnp.float32),
+        pltpu.VMEM((pulses // 8, LANES), jnp.float32),
         pltpu.VMEM((patches, tile), jnp.float32),
         pltpu.VMEM((patches, tile), jnp.float32),
         pltpu.VMEM((patches, tile), jnp.float32),
         pltpu.VMEM((patches, tile), jnp.float32),
-    ] + [pltpu.SemaphoreType.DMA((8,))] + [pltpu.SemaphoreType.DMA] * 6
+    ] + [
+        pltpu.SemaphoreType.DMA((8,)),
+        pltpu.SemaphoreType.DMA,
+        pltpu.SemaphoreType.DMA((pulses // LANES,)),
+    ] + [pltpu.SemaphoreType.DMA] * 4
     shapes = (
         jax.ShapeDtypeStruct((pulses, breadth // devices), jnp.bfloat16),
         jax.ShapeDtypeStruct((patches, tile), jnp.float32),

time: 18.6 us -> 18.5 us (level)
  no operation moved by 1% of the time
where the time goes in v5:
time: 18.5 us; the launch traced here: 18.3 us
  Pallas kernels  16.4 us (89%)
  local copies, waits for them, and re-layouts  1.27 us (7%)
  between operations  0.64 us (3%)
    pallas_call x1, Pallas kernels, body(): pl.pallas_call(functools.partial(kernel, devices, across), out_shape=shap...  16.4 us
    unnamed x2, local copies, waits for them, and re-layouts  1.27 us

profile of v5, /device:TPU:1, one launch (start us, length us, event | category | flops | bytes accessed | tf_op | source)
XLA Modules:
  0.0 18.3 jit_solution(2814780273475767219)
XLA Ops:
  0.6 16.4 %shard_map.95 = (bf16[512,128]{1,0:T(8,128)(2,1)S(1)}, f32[8,1024]{1,0:T(8,128)S(1)}) custom-call(bf16[16,4096]{1,0:T(8,128)(2,1)} %raw_in.1, bf16[2,2048]{1,0:T(2,128)(2,1)} %bitcast.11, s32[1,2048]{1,0:T(1,128)} %bitcast.12, s32[1,2048]{1,0:T(1,128)} %bitcast.13, bf16[8,16]{1,0:T(8,128)(2,1)} %bitcast.15, bf16[2,1024]{1,0:T(2,128)(2,1)} %bitcast.14, ...), custom_call_target="tpu_custom_call" | custom-call | tf_op jit(solution)/shard_map/pallas_call | solution.py:458
  17.0 0.7 %copy.12 = bf16[512,128]{1,0:T(8,128)(2,1)} copy(bf16[512,128]{1,0:T(8,128)(2,1)S(1)} %get-tuple-element.4) | data formatting | bytes 262144
  17.7 0.6 %copy.13 = f32[8,1024]{1,0:T(8,128)} copy(f32[8,1024]{1,0:T(8,128)S(1)} %get-tuple-element.5) | data formatting | bytes 65536

commit v6 on v5

--- a/solution.py
+++ b/solution.py
@@ -11,7 +11,7 @@
 PROWS = 16
 LANES = 128
 GROUP = 16
-BATCH = 4
+BATCH = 16
 MESH = pl.DeviceIdType.MESH
 
 
@@ -338,8 +338,18 @@
             total += weights[:, patch : patch + 1] * looked[patch : patch + 1, :]
         return total
 
-    low_ref[...] = tile_sums(0)
-    high_ref[...] = tile_sums(2 * patches)
+    half_tile = looked.shape[1] // 2
+
+    def packed(total):
+        halves = [total[:, :half_tile], total[:, half_tile:]]
+        return jnp.concatenate(halves, 0).astype(jnp.bfloat16)
+
+    def unpacked(ref):
+        total = ref[...].astype(jnp.float32)
+        return jnp.concatenate([total[:patches], total[patches:]], 1)
+
+    low_ref[...] = packed(tile_sums(0))
+    high_ref[...] = packed(tile_sums(2 * patches))
 
     def low_copy():
         return pltpu.make_async_remote_copy(
@@ -385,12 +395,12 @@
     @pl.when(me < devices - 1)
     def _():
         low_copy().wait_recv()
-        tiles_ref[...] += from_next_ref[...]
+        tiles_ref[...] += unpacked(from_next_ref)
 
     @pl.when(me > 0)
     def _():
         high_copy().wait_recv()
-        tiles_ref[...] += from_prev_ref[...]
+        tiles_ref[...] += unpacked(from_prev_ref)
 
     @pl.when(me > 0)
     def _():
@@ -441,10 +451,10 @@
         pltpu.VMEM((pulses, LANES), jnp.bfloat16),
         pltpu.VMEM((pulses // LANES, 2 * LANES, LANES), jnp.float32),
         pltpu.VMEM((pulses // 8, LANES), jnp.float32),
-        pltpu.VMEM((patches, tile), jnp.float32),
-        pltpu.VMEM((patches, tile), jnp.float32),
-        pltpu.VMEM((patches, tile), jnp.float32),
-        pltpu.VMEM((patches, tile), jnp.float32),
+        pltpu.VMEM((2 * patches, tile // 2), jnp.bfloat16),
+        pltpu.VMEM((2 * patches, tile // 2), jnp.bfloat16),
+        pltpu.VMEM((2 * patches, tile // 2), jnp.bfloat16),
+        pltpu.VMEM((2 * patches, tile // 2), jnp.bfloat16),
     ] + [
         pltpu.SemaphoreType.DMA((8,)),
         pltpu.SemaphoreType.DMA,

time: 18.5 us -> 18 us (0.973)
  Pallas kernels: 16.4 us -> 15.9 us
    pallas_call x1, Pallas kernels: 16.4 us -> 15.9 us  [body(): pl.pallas_call(functools.partial(kernel, devices, across), out_shape=shap...]
where the time goes in v6:
time: 18 us; the launch traced here: 17.8 us
  Pallas kernels  15.9 us (88%)
  local copies, waits for them, and re-layouts  1.27 us (7%)
  between operations  0.64 us (4%)
    pallas_call x1, Pallas kernels, body(): pl.pallas_call(functools.partial(kernel, devices, across), out_shape=shap...  15.9 us
    unnamed x2, local copies, waits for them, and re-layouts  1.27 us

profile of v6, /device:TPU:1, one launch (start us, length us, event | category | flops | bytes accessed | tf_op | source)
XLA Modules:
  0.0 17.8 jit_solution(13099405101812663295)
XLA Ops:
  0.6 15.9 %shard_map.95 = (bf16[512,128]{1,0:T(8,128)(2,1)S(1)}, f32[8,1024]{1,0:T(8,128)S(1)}) custom-call(bf16[16,4096]{1,0:T(8,128)(2,1)} %raw_in.1, bf16[2,2048]{1,0:T(2,128)(2,1)} %bitcast.11, s32[1,2048]{1,0:T(1,128)} %bitcast.12, s32[1,2048]{1,0:T(1,128)} %bitcast.13, bf16[8,16]{1,0:T(8,128)(2,1)} %bitcast.15, bf16[2,1024]{1,0:T(2,128)(2,1)} %bitcast.14, ...), custom_call_target="tpu_custom_call" | custom-call | tf_op jit(solution)/shard_map/pallas_call | solution.py:468
  16.5 0.7 %copy.12 = bf16[512,128]{1,0:T(8,128)(2,1)} copy(bf16[512,128]{1,0:T(8,128)(2,1)S(1)} %get-tuple-element.4) | data formatting | bytes 262144
  17.2 0.6 %copy.13 = f32[8,1024]{1,0:T(8,128)} copy(f32[8,1024]{1,0:T(8,128)S(1)} %get-tuple-element.5) | data formatting | bytes 65536

commit v7 on v6

--- a/solution.py
+++ b/solution.py
@@ -411,6 +411,17 @@
         high_copy().wait_send()
 
 
+def hand_out(focused_ref, tiles_ref, focused_out, tiles_out, sems):
+    copies = (
+        pltpu.make_async_copy(focused_ref, focused_out, sems.at[0]),
+        pltpu.make_async_copy(tiles_ref, tiles_out, sems.at[1]),
+    )
+    for copy in copies:
+        copy.start()
+    for copy in copies:
+        copy.wait()
+
+
 def body(
     raw_echoes, range_taps, mig_offset, interp_band, interp_table, azimuth_taps, geo_list, geo_frac
 ):
@@ -465,7 +476,7 @@
         jax.ShapeDtypeStruct((patches, tile), jnp.float32),
     )
     outside = pl.BlockSpec(memory_space=pltpu.HBM)
-    return pl.pallas_call(
+    results = pl.pallas_call(
         functools.partial(kernel, devices, across),
         out_shape=shapes,
         in_specs=[outside] * 8,
@@ -475,6 +486,13 @@
             collective_id=0, has_side_effects=True, vmem_limit_bytes=40 * 2**20
         ),
     )(*[pltpu.with_memory_space_constraint(operand, pltpu.HBM) for operand in operands])
+    return pl.pallas_call(
+        hand_out,
+        out_shape=shapes,
+        in_specs=[whole] * 2,
+        out_specs=(outside, outside),
+        scratch_shapes=[pltpu.SemaphoreType.DMA((2,))],
+    )(*[pltpu.with_memory_space_constraint(result, pltpu.VMEM) for result in results])
 
 
 def solution(mesh):

time: 18 us -> 17.4 us (0.967)
  local copies, waits for them, and re-layouts: 1.27 us -> 0 us
  Pallas kernels: 15.9 us -> 16.6 us
    unnamed x2 -> x0, local copies, waits for them, and re-layouts: 1.27 us -> none
    pallas_call x0 -> x1, Pallas kernels: none -> 0.68 us  [body(): pl.pallas_call(hand_out, out_shape=shapes, in_specs=[whole] * 2, out_spec...]
where the time goes in v7:
time: 17.4 us; the launch traced here: 17.2 us
  Pallas kernels  16.6 us (95%)
  between operations  0.64 us (4%)
    pallas_call x1, Pallas kernels, body(): pl.pallas_call(functools.partial(kernel, devices, across), out_shape=shap...  15.9 us
    pallas_call x1, Pallas kernels, body(): pl.pallas_call(hand_out, out_shape=shapes, in_specs=[whole] * 2, out_spec...  0.68 us

profile of v7, /device:TPU:1, one launch (start us, length us, event | category | flops | bytes accessed | tf_op | source)
XLA Modules:
  0.0 17.2 jit_solution(5657730175395869520)
XLA Ops:
  0.6 15.9 %shard_map.95 = (bf16[512,128]{1,0:T(8,128)(2,1)S(1)}, f32[8,1024]{1,0:T(8,128)S(1)}) custom-call(bf16[16,4096]{1,0:T(8,128)(2,1)} %raw_in.1, bf16[2,2048]{1,0:T(2,128)(2,1)} %bitcast.11, s32[1,2048]{1,0:T(1,128)} %bitcast.12, s32[1,2048]{1,0:T(1,128)} %bitcast.13, bf16[8,16]{1,0:T(8,128)(2,1)} %bitcast.15, bf16[2,1024]{1,0:T(2,128)(2,1)} %bitcast.14, ...), custom_call_target="tpu_custom_call" | custom-call | tf_op jit(solution)/shard_map/pallas_call | solution.py:479
  16.5 0.7 %shard_map.96 = (bf16[512,128]{1,0:T(8,128)(2,1)}, f32[8,1024]{1,0:T(8,128)}) custom-call(bf16[512,128]{1,0:T(8,128)(2,1)S(1)} %get-tuple-element.4.focused_ref, f32[8,1024]{1,0:T(8,128)S(1)} %get-tuple-element.5.tiles_ref), custom_call_target="tpu_custom_call" | custom-call | tf_op jit(solution)/shard_map/pallas_call | solution.py:489

commit v8 on v7

--- a/solution.py
+++ b/solution.py
@@ -111,10 +111,8 @@
             )
         )
     ]
-    first_copies = (rtaps_copy, offset_copy, band_copy, table_copy, raw_copy)
+    first_copies = (rtaps_copy, raw_copy, offset_copy, band_copy, table_copy)
     later_copies = (ataps_copy, list_copy, frac_copy)
-    rtaps_copy.start()
-    raw_copy.start()
 
     def place(index):
         return (lax.div(index, across), lax.rem(index, across))
@@ -131,7 +129,7 @@
             greet(distance, 0)
     else:
         lax.fori_loop(1, devices, greet, 0)
-    for copy in (offset_copy, band_copy, table_copy) + later_copies:
+    for copy in first_copies + later_copies:
         copy.start()
 
     def each_group(body):
@@ -349,7 +347,6 @@
         return jnp.concatenate([total[:patches], total[patches:]], 1)
 
     low_ref[...] = packed(tile_sums(0))
-    high_ref[...] = packed(tile_sums(2 * patches))
 
     def low_copy():
         return pltpu.make_async_remote_copy(
@@ -374,6 +371,8 @@
     @pl.when(me > 0)
     def _():
         low_copy().start()
+
+    high_ref[...] = packed(tile_sums(2 * patches))
 
     @pl.when(me < devices - 1)
     def _():

time: 17.4 us -> 17.4 us (level)
  no operation moved by 1% of the time
where the time goes in v8:
time: 17.4 us; the launch traced here: 17.2 us
  Pallas kernels  16.5 us (95%)
  between operations  0.64 us (4%)
    pallas_call x1, Pallas kernels, body(): pl.pallas_call(functools.partial(kernel, devices, across), out_shape=shap...  15.9 us
    pallas_call x1, Pallas kernels, body(): pl.pallas_call(hand_out, out_shape=shapes, in_specs=[whole] * 2, out_spec...  0.68 us

profile of v8, /device:TPU:1, one launch (start us, length us, event | category | flops | bytes accessed | tf_op | source)
XLA Modules:
  0.0 17.2 jit_solution(1891711763516409844)
XLA Ops:
  0.6 15.9 %shard_map.95 = (bf16[512,128]{1,0:T(8,128)(2,1)S(1)}, f32[8,1024]{1,0:T(8,128)S(1)}) custom-call(bf16[16,4096]{1,0:T(8,128)(2,1)} %raw_in.1, bf16[2,2048]{1,0:T(2,128)(2,1)} %bitcast.11, s32[1,2048]{1,0:T(1,128)} %bitcast.12, s32[1,2048]{1,0:T(1,128)} %bitcast.13, bf16[8,16]{1,0:T(8,128)(2,1)} %bitcast.15, bf16[2,1024]{1,0:T(2,128)(2,1)} %bitcast.14, ...), custom_call_target="tpu_custom_call" | custom-call | tf_op jit(solution)/shard_map/pallas_call | solution.py:478
  16.5 0.7 %shard_map.96 = (bf16[512,128]{1,0:T(8,128)(2,1)}, f32[8,1024]{1,0:T(8,128)}) custom-call(bf16[512,128]{1,0:T(8,128)(2,1)S(1)} %get-tuple-element.4.focused_ref, f32[8,1024]{1,0:T(8,128)S(1)} %get-tuple-element.5.tiles_ref), custom_call_target="tpu_custom_call" | custom-call | tf_op jit(solution)/shard_map/pallas_call | solution.py:488
